TPU v7x, 256 devices: a whole 4x4x8 slice. The times are simulated.
256 devices in a mesh: rep: 16 (over y, x_hi, core), fsdp: 16 (over z, x_lo).
Axes of the slice: x: 4 (x_hi: 2, x_lo: 2; x = x_hi * 2 + x_lo), y: 4, z: 8, core: 2. Of those that a mesh axis runs over, the one named last changes fastest.
Arguments:
- layer_input: bfloat16 [49152, 8192], P(('rep', 'fsdp')), may hold values from -180 to 180
- queries: bfloat16 [49152, 4096], P(('rep', 'fsdp')), may hold values from -5 to 5
- rotated_key_heads: bfloat16 [49152, 512], P(('rep', 'fsdp')), may hold values from -5 to 5
- context_gradient: bfloat16 [49152, 4096], P(('rep', 'fsdp')), may hold values from -90 to 90
- value_weight: bfloat16 [8192, 512], P('fsdp'), may hold values from -0.049718446 to 0.049718446
Outputs:
- value_grad: bfloat16 [8192, 512], P('fsdp')
- input_grad: bfloat16 [49152, 8192], P(('rep', 'fsdp'))
- peaks: float32 [2], replicated
- weight_magnitude: float32 [1], replicated
All inputs are finite; a program needn't handle non-finite values.
Results may differ from a plain program's by a relative error of at most 0.03.
Values may be sent and summed in bfloat16 or wider, within the bound.
A program may use at most 128 MiB of HBM per device.

v0:
```python
import math

import jax
import jax.numpy as jnp
from jax import lax
from jax.sharding import PartitionSpec as P

HEAD_SIZE = 128
QUERY_HEADS = 32
KEY_VALUE_HEADS = 4


FORWARD_TOP = 448.0
BACKWARD_TOP = 57344.0


def value_cotangent(queries, rotated_key_heads, context_gradient):
    sequence_length = queries.shape[0]
    heads_per_group = QUERY_HEADS // KEY_VALUE_HEADS
    query_layout = queries.reshape(sequence_length, KEY_VALUE_HEADS, heads_per_group, HEAD_SIZE)
    key_layout = rotated_key_heads.reshape(sequence_length, KEY_VALUE_HEADS, HEAD_SIZE)
    gradient_view = context_gradient.reshape(
        sequence_length, KEY_VALUE_HEADS, heads_per_group, HEAD_SIZE
    )
    scores = jnp.einsum(
        "qagd,sad->agqs", query_layout, key_layout, preferred_element_type=jnp.float32
    ) * (1.0 / math.sqrt(HEAD_SIZE))
    position = jnp.arange(sequence_length)
    causal = position[None, :] <= position[:, None]
    scores = jnp.where(causal, scores, -jnp.inf)
    row_peak = jnp.max(scores, axis=-1, keepdims=True)
    expo = jnp.exp(scores - row_peak)
    probability = (expo / jnp.sum(expo, axis=-1, keepdims=True)).astype(jnp.bfloat16)
    backward_cotangent = jnp.einsum(
        "agqs,qagd->sad", probability, gradient_view, preferred_element_type=jnp.float32
    )
    return backward_cotangent.reshape(sequence_length, KEY_VALUE_HEADS * HEAD_SIZE)


def body(layer_input, queries, rotated_key_heads, context_gradient, value_weight):
    replicas = lax.axis_size("rep")
    groups = lax.axis_size("fsdp")
    devices = replicas * groups
    local_input = jnp.max(jnp.abs(layer_input)).astype(jnp.float32)
    local_weight = jnp.max(jnp.abs(value_weight)).astype(jnp.float32)
    peak_input, peak_weight = lax.pmax((local_input, local_weight), ("rep", "fsdp"))
    unit_input = (peak_input + 1e-06) / FORWARD_TOP
    unit_weight = (peak_weight + 1e-06) / FORWARD_TOP
    coded_input = (layer_input.astype(jnp.float32) / unit_input).astype(jnp.bfloat16)
    coded_weight = (value_weight.astype(jnp.float32) / unit_weight).astype(jnp.bfloat16)
    backward_cotangent = value_cotangent(queries, rotated_key_heads, context_gradient)
    peak_grad = lax.pmax(jnp.max(jnp.abs(backward_cotangent)), ("rep", "fsdp"))
    unit_grad = (peak_grad + 1e-06) / BACKWARD_TOP
    coded_grad = (backward_cotangent / unit_grad).astype(jnp.bfloat16)
    input_unit = unit_grad * unit_weight
    product = lax.dot_general(
        coded_grad,
        lax.all_gather(coded_weight, "fsdp", axis=0, tiled=True),
        (((1,), (1,)), ((), ())),
        preferred_element_type=jnp.float32,
    )
    input_grad = (product * input_unit).astype(jnp.bfloat16)
    factor = unit_input * unit_grad / devices
    product = lax.dot_general(
        coded_input, coded_grad, (((0,), (0,)), ((), ())), preferred_element_type=jnp.float32
    )
    group_sum = lax.psum_scatter(
        (product * factor).astype(jnp.bfloat16), "fsdp", scatter_dimension=0, tiled=True
    )
    value_grad = lax.psum(group_sum, "rep")
    peaks = jnp.stack([peak_input, peak_grad])
    weight_magnitude = jnp.reshape(peak_weight, (1,))
    return (value_grad, input_grad, peaks, weight_magnitude)


def solution(mesh):
    return jax.shard_map(
        body,
        mesh=mesh,
        in_specs=(
            P(("rep", "fsdp"), None),
            P(("rep", "fsdp"), None),
            P(("rep", "fsdp"), None),
            P(("rep", "fsdp"), None),
            P("fsdp", None),
        ),
        out_specs=(P("fsdp", None), P(("rep", "fsdp"), None), P(), P()),
        check_vma=False,
    )
```

profile of v0, /device:TPU:1, one launch (start us, length us, event | category | flops | bytes accessed | tf_op | source)
XLA Modules:
  0.0 629.0 jit_solution(5693564895091058310)
XLA Ops:
  7.2 0.0 copy-start.1
  7.2 0.0 reduce-scatter.2.cloned.1.call-start
  7.3 1.8 copy.21
  9.0 1.0 reshape.26
  10.0 1.7 copy.22
  11.8 2.9 abs_reduce_fusion
  14.7 0.0 copy-done.1
  14.7 0.7 abs_reduce_fusion.1
  15.4 1.0 fusion.9
  16.4 1.9 fusion.22
  18.3 0.0 copy-start
  18.4 2.3 abs_reduce_fusion.2
  20.6 81.6 %all-reduce = (f32[]{:T(128)}, f32[]{:T(128)}, f32[]{:T(128)}) all-reduce(bf16[]{:T(256)} %abs_reduce_fusion, f32[]{:T(128)} %get-tuple-element.9, bf16[]{:T(256)} %abs_reduce_fusion.1), channel_id=1, replica_groups=mesh['rep'=16,'fsdp'=16] {'rep','fsdp'}, use_global_device_ids=true, to_apply=%region_1.0 | all-reduce | flops 3 | bytes 20 | tf_op jit(solution)/shard_map/pmax | solution.py:46
  103.5 0.0 copy-done
  103.5 5.6 multiply_convert_fusion
  109.1 0.0 copy-start.2
  109.1 0.0 reduce-scatter.2.cloned.1.call-update
  109.1 0.0 all-gather.2.cloned.1.call-start
  109.9 0.3 copy-done.2
  110.2 0.9 divide_convert_fusion.6
  111.0 0.0 all-gather.2.cloned.1.call-update
  111.1 0.0 all-reduce.3.cloned.1.call-start
  111.1 1.8 pad_maximum_fusion
  113.0 174.6 %reduce-scatter.2.cloned.1.call-done = bf16[512,512]{1,0:T(8,128)(2,1)} async-done(((bf16[8192,512]{1,0:T(8,128)(2,1)}), bf16[512,512]{1,0:T(8,128)(2,1)}) %reduce-scatter.2.cloned.1.call-update) | async-done | bytes 524304 | tf_op jit(solution)/shard_map/reduce_scatter | solution.py:67
  287.6 0.0 all-reduce.3.cloned.1.call-update
  287.6 185.7 %all-gather.2.cloned.1.call-done = bf16[8192,512]{1,0:T(8,128)(2,1)} async-done(((bf16[512,512]{1,0:T(8,128)(2,1)}), bf16[8192,512]{1,0:T(8,128)(2,1)}) %all-gather.2.cloned.1.call-update) | async-done | bytes 8388624 | tf_op jit(solution)/shard_map/all_gather | solution.py:58
  473.3 7.9 %fusion.1 = bf16[192,8192]{1,0:T(8,128)(2,1)} fusion(bf16[8192,512]{1,0:T(8,128)(2,1)} %all-gather.2.cloned.1.call-done, f32[]{:T(128)S(6)} %mul.36, f32[4,192,128]{2,1,0:T(8,128)S(1)} %get-tuple-element.10, f32[]{:T(128)S(6)} %div.45), kind=kOutput, calls=%fused_computation.3 | convolution fusion | flops 1613955072 | bytes 11927560 | tf_op jit(solution)/shard_map/dot_general | solution.py:56
  481.2 139.4 %all-reduce.3.cloned.1.call-done = bf16[512,512]{1,0:T(8,128)(2,1)} async-done(((bf16[512,512]{1,0:T(8,128)(2,1)}), bf16[512,512]{1,0:T(8,128)(2,1)}) %all-reduce.3.cloned.1.call-update) | async-done | bytes 524304 | tf_op jit(solution)/shard_map/psum | solution.py:70
  620.6 1.9 copy.42
  (1 shorter events, 0.0 us)
Async XLA Ops:
  7.2 7.5 %copy-start.1 = (bf16[512,512]{1,0:T(8,128)(2,1)S(1)}, bf16[512,512]{1,0:T(8,128)(2,1)}, u32[]{:S(2)}) copy-start(bf16[512,512]{1,0:T(8,128)(2,1)} %param.9) | copy-start | bytes 1572868
  7.2 280.4 %reduce-scatter.2.cloned.1.call-start = ((), (), s32[]{:S(2)}) async-start(), calls=%async_computation.1 | async-start | bytes 8912896 | tf_op jit(solution)/shard_map/reduce_scatter | solution.py:67
  18.3 85.1 %copy-start = (bf16[192,8192]{1,0:T(8,128)(2,1)S(1)}, bf16[192,8192]{1,0:T(8,128)(2,1)}, u32[]{:S(2)}) copy-start(bf16[192,8192]{1,0:T(8,128)(2,1)} %param.5) | copy-start | bytes 9437188
  109.1 1.1 copy-start.2
  109.1 364.1 %all-gather.2.cloned.1.call-start = ((), (), s32[]{:S(2)}) async-start(), calls=%async_computation.3 | async-start | bytes 8912896 | tf_op jit(solution)/shard_map/all_gather | solution.py:58
  111.1 509.6 %all-reduce.3.cloned.1.call-start = ((), (), s32[]{:S(2)}) async-start(), calls=%async_computation.2 | async-start | bytes 1048576 | tf_op jit(solution)/shard_map/psum | solution.py:70
Sparse Core Ops, SparseCore 0:
  109.2 178.2 reduce-scatter.1
  289.9 183.2 all-gather.1
  475.9 144.6 all-reduce.2
where the time goes:
time: 629 us
  waiting for transfers between devices  500 us (79%)
  blocking collectives  81.6 us (13%)
  matrix products  16.8 us (3%)
  between operations  15.8 us (3%)
  other arithmetic  8.27 us (1%)
  local copies, waits for them, and re-layouts  6.68 us (1%)
    all_gather x1, waiting for transfers between devices, body(): lax.all_gather(coded_weight, 'fsdp', axis=0, tiled=True)  186 us
    reduce_scatter x1, waiting for transfers between devices, body(): lax.psum_scatter((product * factor).astype(jnp.bfloat16), 'fsdp', scatter...  175 us
    psum x1, waiting for transfers between devices, body(): value_grad = lax.psum(group_sum, 'rep')  139 us
    pmax x1, blocking collectives, body(): lax.pmax((local_input, local_weight), ('rep', 'fsdp'))  81.6 us
  transfers between devices with their start and end apart: 3, of which 3 were waited for; matrix products, arithmetic and copies ran while one was open for 2% of the time, Pallas kernels for 0%

commit v1 on v0

v1 whole, which is shorter than its diff:
```python
import functools
import math

import jax
import jax.numpy as jnp
from jax import lax
from jax.experimental import pallas as pl
from jax.experimental.pallas import tpu as pltpu
from jax.sharding import PartitionSpec as P

HEAD = 128
QUERY_HEADS = 32
KV_HEADS = 4
PER_KV = QUERY_HEADS // KV_HEADS
T = 192
D = 8192
KV = KV_HEADS * HEAD
FORWARD_TOP = 448.0
BACKWARD_TOP = 57344.0
MESH = pl.DeviceIdType.MESH
F32 = jnp.float32
BF16 = jnp.bfloat16
NX, NY, NZ = 4, 4, 8


def place(x, y, z, c):
    x = lax.rem(x + NX, NX)
    y = lax.rem(y + NY, NY)
    z = lax.rem(z + NZ, NZ)
    c = lax.rem(c, 2)
    return ((y * 2 + x // 2) * 2 + c, z * 2 + lax.rem(x, 2))


LINE = [(dx, dc) for dx in range(NX) for dc in range(2) if (dx, dc) != (0, 0)]
GROUP = [(dx, dy) for dx in (0, 2) for dy in range(NY) if (dx, dy) != (0, 0)]
PARTNERS = sorted(
    set((dx, 0, 0, dc) for dx, dc in LINE)
    | set((0, dy, 0, 0) for dy in range(1, NY))
    | set((0, 0, dz, 0) for dz in range(1, NZ))
    | set((dx, dy, 0, 0) for dx, dy in GROUP)
)


class Ring:
    def __init__(self, plus, minus, take, bufs, send, recv, width):
        self.plus, self.minus, self.take, self.width = plus, minus, take, width
        self.bufs, self.send, self.recv = bufs, send, recv
        self.copies = []

    def go(self, src, slot, to):
        copy = pltpu.make_async_remote_copy(
            src_ref=src, dst_ref=self.bufs.at[slot], send_sem=self.send.at[slot],
            recv_sem=self.recv.at[slot], device_id=to, device_id_type=MESH,
        )
        copy.start()
        self.copies.append(copy)

    def arrived(self, slot):
        pltpu.make_async_copy(self.bufs.at[slot], self.bufs.at[slot], self.recv.at[slot]).wait()

    def first(self, part):
        if part == 0:
            self.go(self.take(0, 2), 0, self.plus)
            self.go(self.take(0, -1), 2, self.minus)
        else:
            self.go(self.take(1, 2), 1, self.minus)
            self.go(self.take(1, 1), 3, self.plus)

    def second(self, part):
        step = 1 if part == 0 else -1
        self.arrived(part)
        mine = self.take(part, step)

        def add(i, _):
            mine[i] = (mine[i].astype(F32) + self.bufs[part, i].astype(F32)).astype(BF16)
            return 0

        lax.fori_loop(0, 4, add, 0)
        self.go(mine, 4 + part, self.plus if part == 0 else self.minus)

    def finish(self, part, put):
        self.arrived(2 + part)
        self.arrived(4 + part)
        mine = self.take(part, 0)

        def add(i, _):
            total = mine[i].astype(F32) + self.bufs[2 + part, i].astype(F32)
            put(4 * part + i, total + self.bufs[4 + part, i].astype(F32))
            return 0

        lax.fori_loop(0, 4, add, 0)

    def drain(self):
        for copy in self.copies:
            copy.wait_send()


def kernel(
    x_hbm, q_hbm, k_hbm, g_hbm, w_hbm,
    value_hbm, grad_hbm, peak_out,
    xh, q_v, k_v, g_v, wfull, cot, coded, coded_t,
    part_v, xbuf1, ybuf2, fin, r1, r2, r3, r4, zrecv, piece, piece_all, vout,
    mine_v, other_v, pk, pk1, pk2, pk3,
    load_sem, xown_sem, xs_sem, xr_sem, wown_sem, ax_s, ax_r, az_s, az_r,
    cot_s, cot_r, p1s, p1r, p2s, p2r, p3s, p3r,
    r1s, r1r, r2s, r2r, r3s, r3r, r4s, r4r, zs, zr, cs, cr, own_o, oth_s, oth_r, v_o, v_s, v_r,
):
    rep, fsdp = lax.axis_index("rep"), lax.axis_index("fsdp")
    c = lax.rem(rep, 2)
    xhi = lax.rem(rep // 2, 2)
    y = rep // 4
    xlo = lax.rem(fsdp, 2)
    z = fsdp // 2
    x = 2 * xhi + xlo
    xot = 1 - xlo

    def at(dx=0, dy=0, dz=0, dc=0):
        return place(x + dx, y + dy, z + dz, c + dc)

    mate = at(dc=1)
    barrier = pltpu.get_barrier_semaphore()
    for partner in PARTNERS:
        pl.semaphore_signal(barrier, inc=1, device_id=at(*partner), device_id_type=MESH)

    loads = [pltpu.make_async_copy(k_hbm, k_v, load_sem.at[8])]
    for a in range(KV_HEADS):
        cols = pl.ds(a * PER_KV * HEAD, PER_KV * HEAD)
        loads.append(pltpu.make_async_copy(q_hbm.at[:, cols], q_v.at[:, cols], load_sem.at[a]))
        loads.append(pltpu.make_async_copy(g_hbm.at[:, cols], g_v.at[:, cols], load_sem.at[4 + a]))
    for copy in loads:
        copy.start()
    w_half = w_hbm.at[pl.ds(pl.multiple_of(c * 256, 256), 256), :]
    w_own = pltpu.make_async_copy(w_half, wfull.at[fsdp], wown_sem)
    w_own.start()

    def half_cols(f, half):
        return x_hbm.at[:, pl.ds(pl.multiple_of(f * 512 + half * 256, 256), 256)]

    def x_own(f):
        return pltpu.make_async_copy(half_cols(f, c), xh.at[f, pl.ds(0, T), :], xown_sem.at[f])

    def x_swap(f):
        return pltpu.make_async_remote_copy(
            src_ref=half_cols(f, 1 - c), dst_ref=xh.at[f, pl.ds(T, T), :], send_sem=xs_sem.at[f],
            recv_sem=xr_sem.at[f], device_id=mate, device_id_type=MESH,
        )

    lax.fori_loop(0, 16, lambda f, _: (x_own(f).start(), 0)[1], 0)

    key_pos = lax.broadcasted_iota(jnp.int32, (T, 2 * T), 0)
    query_pos = lax.broadcasted_iota(jnp.int32, (T, 2 * T), 1)
    keep = key_pos <= jnp.where(query_pos >= T, query_pos - T, query_pos)

    def attention(a):
        if a == 0:
            loads[0].wait()
        loads[1 + 2 * a].wait()
        loads[2 + 2 * a].wait()
        keys = k_v[:, a * HEAD:(a + 1) * HEAD]
        total = jnp.zeros((T, HEAD), F32)
        for pair in range(PER_KV // 2):
            base = (a * PER_KV + 2 * pair) * HEAD
            qs = jnp.concatenate([q_v[:, base:base + HEAD], q_v[:, base + HEAD:base + 2 * HEAD]], axis=0)
            gs = jnp.concatenate([g_v[:, base:base + HEAD], g_v[:, base + HEAD:base + 2 * HEAD]], axis=0)
            scores = lax.dot_general(
                keys, qs, (((1,), (1,)), ((), ())), preferred_element_type=F32
            ) * (1.0 / math.sqrt(HEAD))
            scores = jnp.where(keep, scores, -jnp.inf)
            expo = jnp.exp(scores - jnp.max(scores, axis=0, keepdims=True))
            prob = (expo * (1.0 / jnp.sum(expo, axis=0, keepdims=True))).astype(BF16)
            total += jnp.dot(prob, gs, preferred_element_type=F32)
        cot[0, :, a * HEAD:(a + 1) * HEAD] = total

    attention(0)
    pl.semaphore_wait(barrier, len(PARTNERS))

    ax = []
    for i, dx in enumerate((1, -1)):
        rows = pl.ds(128 * i, 128)
        src = w_hbm.at[pl.ds(pl.multiple_of(c * 256 + 128 * i, 128), 128), :]
        ax.append(pltpu.make_async_remote_copy(
            src_ref=src, dst_ref=wfull.at[fsdp, rows, :], send_sem=ax_s.at[i], recv_sem=ax_r.at[i],
            device_id=at(dx=dx), device_id_type=MESH,
        ))
        ax[-1].start()
    az = {}

    def az_slot(way, d, p):
        return (way * 4 + d - 1) * 2 + p

    def az_send(d, p):
        for way, dz in enumerate((1, -1)):
            if d == 4 and p != way:
                continue
            block = lax.rem(z - dz * (d - 1) + NZ, NZ) * 2 + (xlo if p == 0 else xot)
            slot = az_slot(way, d, p)
            src = w_half if d == 1 and p == 0 else wfull.at[block]
            copy = pltpu.make_async_remote_copy(
                src_ref=src, dst_ref=wfull.at[block], send_sem=az_s.at[slot], recv_sem=az_r.at[slot],
                device_id=at(dz=dz), device_id_type=MESH,
            )
            copy.start()
            az[slot] = copy

    def az_wait(d, p):
        for way in range(2):
            if d == 4 and p != way:
                continue
            slot = az_slot(way, d, p)
            pltpu.make_async_copy(wfull.at[0], wfull.at[0], az_r.at[slot]).wait()

    az_send(1, 0)
    lax.fori_loop(0, 16, lambda f, _: (x_swap(f).start(), 0)[1], 0)
    attention(1)
    for i in range(2):
        ax[i].wait_recv()
    az_send(1, 1)
    attention(2)
    attention(3)

    cot_copy = pltpu.make_async_remote_copy(
        src_ref=cot.at[0], dst_ref=cot.at[1], send_sem=cot_s, recv_sem=cot_r,
        device_id=mate, device_id_type=MESH,
    )
    cot_copy.start()

    def x_max(f, top):
        x_own(f).wait()
        x_swap(f).wait_recv()
        return jnp.maximum(top, jnp.max(jnp.abs(xh[f].astype(F32)), axis=0, keepdims=True))

    top_x = lax.fori_loop(0, 16, x_max, jnp.zeros((1, 256), F32))
    top_x = jnp.max(top_x, axis=1, keepdims=True)
    w_own.wait()
    top_w = jnp.max(jnp.max(jnp.abs(wfull[fsdp].astype(F32)), axis=0, keepdims=True), axis=1, keepdims=True)
    top_g = jnp.max(jnp.max(jnp.abs(cot[0]), axis=0, keepdims=True), axis=1, keepdims=True)
    row = lax.broadcasted_iota(jnp.int32, (8, 128), 0)
    pk[0] = jnp.where(row == 0, top_x, jnp.where(row == 1, top_w, top_g))

    pk_copies = []

    def peak_stage(stage, targets, got, s_sem, r_sem):
        for i, to in enumerate(targets):
            copy = pltpu.make_async_remote_copy(
                src_ref=pk.at[stage], dst_ref=got.at[i], send_sem=s_sem.at[i], recv_sem=r_sem.at[i],
                device_id=to, device_id_type=MESH,
            )
            copy.start()
            pk_copies.append(copy)

    def peak_join(stage, count, got, r_sem):
        top = pk[stage]
        for i in range(count):
            pltpu.make_async_copy(got.at[i], got.at[i], r_sem.at[i]).wait()
            top = jnp.maximum(top, got[i])
        pk[stage + 1] = top

    peak_stage(0, [at(dx=dx, dc=dc) for dx, dc in LINE], pk1, p1s, p1r)
    az_wait(1, 0)
    az_send(2, 0)
    peak_join(0, len(LINE), pk1, p1r)
    peak_stage(1, [at(dy=dy) for dy in range(1, NY)], pk2, p2s, p2r)
    peak_join(1, NY - 1, pk2, p2r)
    peak_stage(2, [at(dz=dz) for dz in range(1, NZ)], pk3, p3s, p3r)
    cot_copy.wait_recv()
    peak_join(2, NZ - 1, pk3, p3r)
    az_wait(1, 1)
    az_send(2, 1)
    top = pk[3]
    peak_out[...] = top
    unit_x = (top[0:1, 0:1] + 1e-06) / FORWARD_TOP
    unit_w = (top[1:2, 0:1] + 1e-06) / FORWARD_TOP
    unit_g = (top[2:3, 0:1] + 1e-06) / BACKWARD_TOP
    inv_x, inv_w, inv_g = 1.0 / unit_x, 1.0 / unit_w, 1.0 / unit_g
    input_unit = unit_g * unit_w
    factor = unit_x * unit_g / 256.0
    for i in range(2):
        scaled = cot[i] * inv_g
        coded[pl.ds(T * i, T), :] = scaled.astype(BF16)
    coded_t[...] = jnp.transpose(coded[...].astype(F32)).astype(BF16)

    def product(zd, _):
        for xl in range(2):
            block = (xh[zd * 2 + xl].astype(F32) * inv_x).astype(BF16)
            out = jnp.dot(coded_t[...], block, preferred_element_type=F32) * factor
            part_v[zd, xl] = out.astype(BF16).reshape(2, NY, 64, 256)
        return 0

    def xdest(step):
        xd = lax.rem(x + step + NX, NX)
        return lax.rem(xd, 2), xd // 2

    def ydest(step):
        return lax.rem(y + step + NY, NY)

    def take1(p, step):
        xl, xg = xdest(step)
        return part_v.at[pl.ds(4 * p, 4), xl, xg, :, pl.ds(0, 32), :]

    def take2(p, step):
        return part_v.at[pl.ds(4 * p, 4), :, :, ydest(step), pl.ds(32, 32), :]

    def take3(p, step):
        return xbuf1.at[pl.ds(4 * p, 4), ydest(step)]

    def take4(p, step):
        xl, xg = xdest(step)
        return ybuf2.at[pl.ds(4 * p, 4), xl, xg]

    xp, xm, yp, ym = at(dx=1), at(dx=-1), at(dy=1), at(dy=-1)
    ring1 = Ring(xp, xm, take1, r1, r1s, r1r, 1)
    ring2 = Ring(yp, ym, take2, r2, r2s, r2r, 1)
    ring3 = Ring(yp, ym, take3, r3, r3s, r3r, 1)
    ring4 = Ring(xp, xm, take4, r4, r4s, r4r, 1)

    lax.fori_loop(0, 4, product, 0)
    ring1.first(0)
    ring2.first(0)
    lax.fori_loop(4, 8, product, 0)
    ring1.first(1)
    ring2.first(1)

    def own_out(f):
        return pltpu.make_async_copy(
            mine_v.at[f], grad_hbm.at[:, pl.ds(pl.multiple_of(f * 512 + c * 256, 256), 256)], own_o.at[f]
        )

    def mate_out(f):
        return pltpu.make_async_remote_copy(
            src_ref=other_v.at[f],
            dst_ref=grad_hbm.at[:, pl.ds(pl.multiple_of(f * 512 + c * 256, 256), 256)],
            send_sem=oth_s.at[f], recv_sem=oth_r.at[f], device_id=mate, device_id_type=MESH,
        )

    def input_grad(zb):
        zb = lax.rem(zb + NZ, NZ)

        def one(xl, _):
            f = zb * 2 + xl
            block = (wfull[f].astype(F32) * inv_w).astype(BF16)
            out = lax.dot_general(coded[...], block, (((1,), (1,)), ((), ())), preferred_element_type=F32)
            out = (out * input_unit).astype(BF16)
            mine_v[f] = out[0:T]
            other_v[f] = out[T:2 * T]
            own_out(f).start()
            mate_out(f).start()
            return 0

        lax.fori_loop(0, 2, one, 0)

    input_grad(z)
    az_wait(2, 0)
    az_send(3, 0)
    ring1.second(0)
    ring2.second(0)
    ring1.second(1)
    ring2.second(1)
    input_grad(z - 1)
    input_grad(z + 1)
    az_wait(2, 1)
    az_send(3, 1)

    def put1(i, v):
        xbuf1[i] = v.astype(BF16)

    def put2(i, v):
        ybuf2[i] = v.astype(BF16)

    def put3(i, v):
        fin[i, pl.ds(0, 32), :] = v.astype(BF16)

    def put4(i, v):
        fin[i, pl.ds(32, 32), :] = v.astype(BF16)

    ring1.finish(0, put1)
    ring3.first(0)
    ring2.finish(0, put2)
    ring4.first(0)
    ring1.finish(1, put1)
    ring3.first(1)
    ring2.finish(1, put2)
    ring4.first(1)
    input_grad(z - 2)
    input_grad(z + 2)
    ring3.second(0)
    ring4.second(0)
    ring3.second(1)
    ring4.second(1)
    az_wait(3, 0)
    az_send(4, 0)
    ring3.finish(0, put3)
    ring4.finish(0, put4)
    ring3.finish(1, put3)
    ring4.finish(1, put4)

    z_copies = []
    for i in range(1, NZ):
        zd = lax.rem(z + i, NZ)
        copy = pltpu.make_async_remote_copy(
            src_ref=fin.at[zd], dst_ref=zrecv.at[i], send_sem=zs.at[i], recv_sem=zr.at[i],
            device_id=at(dz=i), device_id_type=MESH,
        )
        copy.start()
        z_copies.append(copy)
    az_wait(3, 1)
    az_send(4, 1)
    input_grad(z - 3)
    input_grad(z + 3)
    total = fin[z].astype(F32)
    for i in range(1, NZ):
        z_copies[i - 1].wait_recv()
        total += zrecv[i].astype(F32)
    j = xhi * NY + y
    piece[...] = total.astype(BF16)

    rows_j = pl.ds(pl.multiple_of(j * 64, 64), 64)
    c_copies = []
    for i, (dx, dy) in enumerate(GROUP):
        copy = pltpu.make_async_remote_copy(
            src_ref=piece, dst_ref=piece_all.at[rows_j, :], send_sem=cs.at[i], recv_sem=cr.at[i],
            device_id=at(dx=dx, dy=dy), device_id_type=MESH,
        )
        copy.start()
        c_copies.append(copy)
    piece_all[rows_j, :] = piece[...]
    az_wait(4, 0)
    az_wait(4, 1)
    input_grad(z + 4)
    for copy in c_copies:
        copy.wait_recv()
    vout[...] = jnp.transpose(piece_all[...].astype(F32)).astype(BF16)
    v_rows = value_hbm.at[pl.ds(pl.multiple_of(c * 256, 256), 256), :]
    v_mine = pltpu.make_async_copy(vout, v_rows, v_o)
    v_mine.start()
    v_mate = pltpu.make_async_remote_copy(
        src_ref=vout, dst_ref=v_rows, send_sem=v_s, recv_sem=v_r, device_id=mate, device_id_type=MESH,
    )
    v_mate.start()

    for copy in ax:
        copy.wait_send()
    for copy in az.values():
        copy.wait_send()
    for copy in pk_copies + z_copies + c_copies + [cot_copy]:
        copy.wait_send()
    for ring in (ring1, ring2, ring3, ring4):
        ring.drain()

    def last(f, _):
        x_swap(f).wait_send()
        own_out(f).wait()
        mate_out(f).wait()
        return 0

    lax.fori_loop(0, 16, last, 0)
    v_mine.wait()
    v_mate.wait()


def body(layer_input, queries, keys, context_gradient, weight):
    dma = pltpu.SemaphoreType.DMA
    vm = pltpu.VMEM
    anywhere = pl.BlockSpec(memory_space=pl.ANY)
    value_grad, input_grad, peaks = pl.pallas_call(
        kernel,
        out_shape=(
            jax.ShapeDtypeStruct((512, KV), BF16),
            jax.ShapeDtypeStruct((T, D), BF16),
            jax.ShapeDtypeStruct((8, 128), F32),
        ),
        in_specs=[anywhere] * 5,
        out_specs=(anywhere, anywhere, pl.BlockSpec(memory_space=pltpu.VMEM)),
        scratch_shapes=[
            vm((16, 2 * T, 256), BF16), vm((T, 4096), BF16), vm((T, KV), BF16), vm((T, 4096), BF16),
            vm((16, 256, KV), BF16), vm((2, T, KV), F32), vm((2 * T, KV), BF16), vm((KV, 2 * T), BF16),
            vm((NZ, 2, 2, NY, 64, 256), BF16), vm((NZ, NY, 32, 256), BF16), vm((NZ, 2, 2, 32, 256), BF16),
            vm((NZ, 64, 256), BF16),
            vm((6, 4, NY, 32, 256), BF16), vm((6, 4, 2, 2, 32, 256), BF16),
            vm((6, 4, 32, 256), BF16), vm((6, 4, 32, 256), BF16),
            vm((NZ, 64, 256), BF16), vm((64, 256), BF16), vm((KV, 256), BF16), vm((256, KV), BF16),
            vm((16, T, 256), BF16), vm((16, T, 256), BF16),
            vm((4, 8, 128), F32), vm((7, 8, 128), F32), vm((3, 8, 128), F32), vm((7, 8, 128), F32),
            dma((9,)), dma((16,)), dma((16,)), dma((16,)), dma, dma((2,)), dma((2,)), dma((16,)), dma((16,)),
            dma, dma, dma((7,)), dma((7,)), dma((3,)), dma((3,)), dma((7,)), dma((7,)),
            dma((6,)), dma((6,)), dma((6,)), dma((6,)), dma((6,)), dma((6,)), dma((6,)), dma((6,)),
            dma((8,)), dma((8,)), dma((7,)), dma((7,)), dma((16,)), dma((16,)), dma((16,)), dma, dma, dma,
        ],
        compiler_params=pltpu.CompilerParams(
            collective_id=0, has_side_effects=True, vmem_limit_bytes=60 << 20
        ),
        name="value_backward",
    )(layer_input, queries, keys, context_gradient, weight)
    return value_grad, input_grad, jnp.stack([peaks[0, 0], peaks[2, 0]]), peaks[1, 0:1]


def solution(mesh):
    return jax.shard_map(
        body,
        mesh=mesh,
        in_specs=(
            P(("rep", "fsdp"), None),
            P(("rep", "fsdp"), None),
            P(("rep", "fsdp"), None),
            P(("rep", "fsdp"), None),
            P("fsdp", None),
        ),
        out_specs=(P("fsdp", None), P(("rep", "fsdp"), None), P(), P()),
        check_vma=False,
    )
```

time: 629 us -> 88 us (0.14)
  waiting for transfers between devices: 500 us -> 0 us
  blocking collectives: 81.6 us -> 0 us
  Pallas kernels: 0 us -> 78.3 us
  matrix products: 16.8 us -> 0 us
  between operations: 15.8 us -> 0.64 us
  other arithmetic: 8.27 us -> 1.88 us
    all_gather x1 -> x0, waiting for transfers between devices: 186 us -> none  [body(): lax.all_gather(coded_weight, 'fsdp', axis=0, tiled=True)]
    reduce_scatter x1 -> x0, waiting for transfers between devices: 175 us -> none  [body(): lax.psum_scatter((product * factor).astype(jnp.bfloat16), 'fsdp', scatter...]
    psum x1 -> x0, waiting for transfers between devices: 139 us -> none  [body(): value_grad = lax.psum(group_sum, 'rep')]
    pmax x1 -> x0, blocking collectives: 81.6 us -> none  [body(): lax.pmax((local_input, local_weight), ('rep', 'fsdp'))]
    pallas_call x0 -> x1, Pallas kernels: none -> 78.3 us  [body(): pl.pallas_call(kernel, out_shape=(jax.ShapeDtypeStruct((512, KV), BF16),...]
    dot_general x4 -> x0, matrix products: 16.8 us -> none  [the longest x1 7.91 us: body(): lax.dot_general(coded_grad, lax.all_gather(coded_weight, 'fsdp', axis=0,...]
  transfers between devices with their start and end apart: 3 -> 0, of which waited for: 3 -> 0; matrix products, arithmetic and copies ran while one was open for 2% -> 0% of each run, Pallas kernels for 0% -> 0%
where the time goes in v1:
time: 88 us; the launch traced here: 87.8 us
  Pallas kernels  78.3 us (89%)
  local copies, waits for them, and re-layouts  7.04 us (8%)
  other arithmetic  1.88 us (2%)
    pallas_call x1, Pallas kernels, body(): pl.pallas_call(kernel, out_shape=(jax.ShapeDtypeStruct((512, KV), BF16),...  78.3 us
    unnamed x2, local copies, waits for them, and re-layouts  5.72 us
    another operation x1, other arithmetic, body(): jnp.stack([peaks[0, 0], peaks[2, 0]])  1.88 us

profile of v1, /device:TPU:1, one launch (start us, length us, event | category | flops | bytes accessed | tf_op | source)
XLA Modules:
  0.0 87.8 jit_solution(7362582571020899202)
XLA Ops:
  0.6 78.3 %value_backward.1 = (bf16[512,512]{1,0:T(8,128)(2,1)}, bf16[192,8192]{1,0:T(8,128)(2,1)}, f32[8,128]{1,0:T(8,128)}) custom-call(bf16[192,8192]{1,0:T(8,128)(2,1)} %x_hbm.1, bf16[192,4096]{1,0:T(8,128)(2,1)} %q_hbm.1, bf16[192,512]{1,0:T(8,128)(2,1)} %k_hbm.1, bf16[192,4096]{1,0:T(8,128)(2,1)} %g_hbm.1, bf16[512,512]{1,0:T(8,128)(2,1)} %w_hbm.1), custom_call_target="tpu_custom_call" | custom-call | tf_op jit(solution)/shard_map/value_backward/pallas_call | solution.py:464
  78.9 1.3 %fusion = (f32[1,1]{1,0:T(1,128)}, f32[1,1]{1,0:T(1,128)}, f32[1,1]{1,0:T(1,128)}) fusion(f32[8,128]{1,0:T(8,128)} %get-tuple-element.9), kind=kLoop, calls=%fused_computation.1 | loop fusion | bytes 24 | tf_op jit(solution)/shard_map/slice | solution.py:493
  80.2 1.9 %pad_maximum_fusion = f32[2]{0:T(128)} fusion(f32[1]{0:T(128)} %bitcast.1, f32[1]{0:T(128)} %bitcast), kind=kLoop, calls=%fused_computation | loop fusion | flops 2 | bytes 16 | tf_op jit(solution)/shard_map/stack | solution.py:493
  82.1 1.9 %copy.11 = bf16[512,512]{1,0:T(8,128)(2,1)} copy(bf16[512,512]{1,0:T(8,128)(2,1)} %get-tuple-element.17) | data formatting | bytes 1048576
  84.0 3.9 %copy.12 = bf16[192,8192]{1,0:T(8,128)(2,1)} copy(bf16[192,8192]{1,0:T(8,128)(2,1)} %get-tuple-element.18) | data formatting | bytes 6291456

commit v2 on v1

v2 whole, which is shorter than its diff:
```python
import functools
import math

import jax
import jax.numpy as jnp
from jax import lax
from jax.experimental import pallas as pl
from jax.experimental.pallas import tpu as pltpu
from jax.sharding import PartitionSpec as P

HEAD = 128
QUERY_HEADS = 32
KV_HEADS = 4
PER_KV = QUERY_HEADS // KV_HEADS
T = 192
D = 8192
KV = KV_HEADS * HEAD
MESH = pl.DeviceIdType.MESH
F32 = jnp.float32
BF16 = jnp.bfloat16
NX, NY, NZ = 4, 4, 8
CUTS = 8


def place(x, y, z, c):
    x = lax.rem(x + NX, NX)
    y = lax.rem(y + NY, NY)
    z = lax.rem(z + NZ, NZ)
    c = lax.rem(c, 2)
    return ((y * 2 + x // 2) * 2 + c, z * 2 + lax.rem(x, 2))


LINE = [(dx, dc) for dx in range(NX) for dc in range(2) if (dx, dc) != (0, 0)]
GROUP = [(dx, dy) for dx in (0, 2) for dy in range(NY) if (dx, dy) != (0, 0)]
PARTNERS = sorted(
    set((dx, 0, 0, dc) for dx, dc in LINE)
    | set((0, dy, 0, 0) for dy in range(1, NY))
    | set((0, 0, dz, 0) for dz in range(1, NZ))
    | set((dx, dy, 0, 0) for dx, dy in GROUP)
)


class Ring:
    def __init__(self, plus, minus, take, put, bufs, send, recv):
        self.plus, self.minus, self.take, self.put = plus, minus, take, put
        self.bufs, self.send, self.recv = bufs, send, recv
        self.copies = []

    def go(self, src, slot, to):
        copy = pltpu.make_async_remote_copy(
            src_ref=src, dst_ref=self.bufs.at[slot], send_sem=self.send.at[slot],
            recv_sem=self.recv.at[slot], device_id=to, device_id_type=MESH,
        )
        copy.start()
        self.copies.append(copy)

    def arrived(self, slot):
        pltpu.make_async_copy(self.bufs.at[slot], self.bufs.at[slot], self.recv.at[slot]).wait()

    def first(self, part):
        if part == 0:
            self.go(self.take(0, 2), 0, self.plus)
            self.go(self.take(0, -1), 2, self.minus)
        else:
            self.go(self.take(1, 2), 1, self.minus)
            self.go(self.take(1, 1), 3, self.plus)

    def second(self, part):
        step = 1 if part == 0 else -1
        self.arrived(part)
        mine = self.take(part, step)

        def add(i, _):
            mine[i] = (mine[i].astype(F32) + self.bufs[part, i].astype(F32)).astype(BF16)
            return 0

        lax.fori_loop(0, 4, add, 0)
        self.go(mine, 4 + part, self.plus if part == 0 else self.minus)

    def finish(self, part):
        self.arrived(2 + part)
        self.arrived(4 + part)
        mine = self.take(part, 0)

        def add(i, _):
            total = mine[i].astype(F32) + self.bufs[2 + part, i].astype(F32)
            self.put(4 * part + i, total + self.bufs[4 + part, i].astype(F32))
            return 0

        lax.fori_loop(0, 4, add, 0)

    def drain(self):
        for copy in self.copies:
            copy.wait_send()


def kernel(
    x_hbm, q_hbm, k_hbm, g_hbm, w_hbm,
    value_hbm, grad_hbm, peak_out,
    xh, q_v, k_v, g_v, wfull, cot, coded_t,
    part_v, xbuf, ybuf, fin, r1, r2, r3, r4, zrecv, piece, piece_all, vout,
    mine_v, other_v, pk, pk1, pk2, pk3,
    load_sem, xown_sem, xs_sem, xr_sem, wown_sem, ax_s, ax_r, az_s, az_r,
    cot_s, cot_r, p1s, p1r, p2s, p2r, p3s, p3r,
    r1s, r1r, r2s, r2r, r3s, r3r, r4s, r4r, zs, zr, cs, cr, own_o, oth_s, oth_r, v_o, v_s, v_r,
):
    rep, fsdp = lax.axis_index("rep"), lax.axis_index("fsdp")
    c = lax.rem(rep, 2)
    xhi = lax.rem(rep // 2, 2)
    y = rep // 4
    xlo = lax.rem(fsdp, 2)
    z = fsdp // 2
    x = 2 * xhi + xlo
    xot = 1 - xlo

    def at(dx=0, dy=0, dz=0, dc=0):
        return place(x + dx, y + dy, z + dz, c + dc)

    mate = at(dc=1)
    barrier = pltpu.get_barrier_semaphore()
    for partner in PARTNERS:
        pl.semaphore_signal(barrier, inc=1, device_id=at(*partner), device_id_type=MESH)

    loads = [pltpu.make_async_copy(k_hbm, k_v, load_sem.at[8])]
    for a in range(KV_HEADS):
        cols = pl.ds(a * PER_KV * HEAD, PER_KV * HEAD)
        loads.append(pltpu.make_async_copy(q_hbm.at[:, cols], q_v.at[:, cols], load_sem.at[a]))
        loads.append(pltpu.make_async_copy(g_hbm.at[:, cols], g_v.at[:, cols], load_sem.at[4 + a]))
    for copy in loads:
        copy.start()
    w_half = w_hbm.at[pl.ds(pl.multiple_of(c * 256, 256), 256), :]
    w_own = pltpu.make_async_copy(w_half, wfull.at[fsdp], wown_sem)
    w_own.start()

    def half_cols(f, half):
        return x_hbm.at[:, pl.ds(pl.multiple_of(f * 512 + half * 256, 256), 256)]

    def x_own(f):
        return pltpu.make_async_copy(half_cols(f, c), xh.at[f, pl.ds(0, T), :], xown_sem.at[f])

    def x_swap(f):
        return pltpu.make_async_remote_copy(
            src_ref=half_cols(f, 1 - c), dst_ref=xh.at[f, pl.ds(T, T), :], send_sem=xs_sem.at[f],
            recv_sem=xr_sem.at[f], device_id=mate, device_id_type=MESH,
        )

    lax.fori_loop(0, 16, lambda f, _: (x_own(f).start(), 0)[1], 0)

    key_pos = lax.broadcasted_iota(jnp.int32, (T, 2 * T), 0)
    query_pos = lax.broadcasted_iota(jnp.int32, (T, 2 * T), 1)
    keep = key_pos <= jnp.where(query_pos >= T, query_pos - T, query_pos)

    def attention(a):
        if a == 0:
            loads[0].wait()
        loads[1 + 2 * a].wait()
        loads[2 + 2 * a].wait()
        keys = k_v[:, a * HEAD:(a + 1) * HEAD]
        total = jnp.zeros((T, HEAD), F32)
        for pair in range(PER_KV // 2):
            base = (a * PER_KV + 2 * pair) * HEAD
            qs = jnp.concatenate([q_v[:, base:base + HEAD], q_v[:, base + HEAD:base + 2 * HEAD]], axis=0)
            gs = jnp.concatenate([g_v[:, base:base + HEAD], g_v[:, base + HEAD:base + 2 * HEAD]], axis=0)
            scores = lax.dot_general(
                keys, qs, (((1,), (1,)), ((), ())), preferred_element_type=F32
            ) * (1.0 / math.sqrt(HEAD))
            scores = jnp.where(keep, scores, -jnp.inf)
            expo = jnp.exp(scores - jnp.max(scores, axis=0, keepdims=True))
            prob = (expo * (1.0 / jnp.sum(expo, axis=0, keepdims=True))).astype(BF16)
            total += jnp.dot(prob, gs, preferred_element_type=F32)
        cot[0, :, a * HEAD:(a + 1) * HEAD] = total.astype(BF16)
        return jnp.max(jnp.abs(total), axis=0, keepdims=True)

    pl.semaphore_wait(barrier, len(PARTNERS))
    lax.fori_loop(0, 16, lambda f, _: (x_swap(f).start(), 0)[1], 0)

    ax = {}

    def across(b, src, block, rows):
        for i, dx in enumerate((1, -1)):
            for k, base in enumerate(rows):
                part = pl.ds(base + 64 * i, 64)
                slot = (b * 2 + k) * 2 + i
                copy = pltpu.make_async_remote_copy(
                    src_ref=src(base + 64 * i), dst_ref=wfull.at[block, part, :],
                    send_sem=ax_s.at[slot], recv_sem=ax_r.at[slot], device_id=at(dx=dx), device_id_type=MESH,
                )
                copy.start()
                ax[slot] = copy

    def across_wait(b, k):
        for i in range(2):
            pltpu.make_async_copy(
                wfull.at[0, pl.ds(0, 64), :], wfull.at[0, pl.ds(0, 64), :], ax_r.at[(b * 2 + k) * 2 + i]
            ).wait()

    def own_rows(base):
        return w_hbm.at[pl.ds(pl.multiple_of(c * 256 + base, 64), 64), :]

    def spread(dz):
        block = lax.rem(z + dz + NZ, NZ) * 2 + xlo
        across(1 + dz % NZ, lambda base: wfull.at[block, pl.ds(base, 64), :], block, (0,))

    az = {}
    WHOLE, LATE, FIRST, LAST = (0, 256), (128, 128), (0, 192), (192, 64)

    def az_list(d, p):
        if d < 4:
            return [(way, 0, WHOLE if p == 0 else LATE) for way in range(2)]
        return [(0, 0, FIRST), (1, 0, LAST)] if p == 0 else [(1, 0, LATE)]

    def az_slot(way, d, p):
        return (way * 4 + d - 1) * 2 + p

    def az_send(d, p):
        for way, _, (base, count) in az_list(d, p):
            dz = 1 - 2 * way
            block = lax.rem(z - dz * (d - 1) + NZ, NZ) * 2 + (xlo if p == 0 else xot)
            slot = az_slot(way, d, p)
            rows = pl.ds(base, count)
            src = w_half if d == 1 and p == 0 else wfull.at[block, rows, :]
            copy = pltpu.make_async_remote_copy(
                src_ref=src, dst_ref=wfull.at[block, rows, :], send_sem=az_s.at[slot], recv_sem=az_r.at[slot],
                device_id=at(dz=dz), device_id_type=MESH,
            )
            copy.start()
            az[slot] = copy

    def az_wait(d, p):
        for way, _, (base, count) in az_list(d, p):
            view = wfull.at[0, pl.ds(base, count), :]
            pltpu.make_async_copy(view, view, az_r.at[az_slot(way, d, p)]).wait()

    cot_copies = []

    def cot_send(s):
        cols = pl.ds(256 * s, 256)
        cot_copies.append(pltpu.make_async_remote_copy(
            src_ref=cot.at[0, :, cols], dst_ref=cot.at[1, :, cols], send_sem=cot_s.at[s], recv_sem=cot_r.at[s],
            device_id=mate, device_id_type=MESH,
        ))
        cot_copies[-1].start()

    pk_copies = []

    def peak_send(stage, targets, got, s_sem, r_sem):
        for i, to in enumerate(targets):
            copy = pltpu.make_async_remote_copy(
                src_ref=pk.at[stage], dst_ref=got.at[i], send_sem=s_sem.at[i], recv_sem=r_sem.at[i],
                device_id=to, device_id_type=MESH,
            )
            copy.start()
            pk_copies.append(copy)

    def peak_join(stage, count, got, r_sem):
        top = pk[stage]
        for i in range(count):
            pltpu.make_async_copy(got.at[i], got.at[i], r_sem.at[i]).wait()
            top = jnp.maximum(top, got[i])
        pk[stage + 1] = top

    def product(s):
        def one(zd, top):
            for xl in range(2):
                f = zd * 2 + xl
                if s == 0:
                    x_own(f).wait()
                    x_swap(f).wait_recv()
                block = xh[f]
                if s == 0:
                    top = jnp.maximum(top, jnp.max(jnp.abs(block.astype(F32)), axis=0, keepdims=True))
                out = jnp.dot(coded_t[...], block, preferred_element_type=F32) * (1.0 / 256.0)
                part_v[s, zd, xl] = out.astype(BF16).reshape(2, 2, NY, 16, 256)
            return top
        return one

    def xdest(step):
        xd = lax.rem(x + step + NX, NX)
        return lax.rem(xd, 2), xd // 2

    def ydest(step):
        return lax.rem(y + step + NY, NY)

    xp, xm, yp, ym = at(dx=1), at(dx=-1), at(dy=1), at(dy=-1)

    def rings(s):
        def take1(p, step):
            xl, xg = xdest(step)
            return part_v.at[s, pl.ds(4 * p, 4), xl, 0, xg]

        def take2(p, step):
            return part_v.at[s, pl.ds(4 * p, 4), :, 1, :, ydest(step)]

        def take3(p, step):
            return xbuf.at[s, pl.ds(4 * p, 4), ydest(step)]

        def take4(p, step):
            xl, xg = xdest(step)
            return ybuf.at[s, pl.ds(4 * p, 4), xl, xg]

        def put1(i, v):
            xbuf[s, i] = v.astype(BF16)

        def put2(i, v):
            ybuf[s, i] = v.astype(BF16)

        def put3(i, v):
            fin[s, i, 0] = v.astype(BF16)

        def put4(i, v):
            fin[s, i, 1] = v.astype(BF16)

        return (
            Ring(xp, xm, take1, put1, r1.at[s], r1s.at[s], r1r.at[s]),
            Ring(yp, ym, take2, put2, r2.at[s], r2s.at[s], r2r.at[s]),
            Ring(yp, ym, take3, put3, r3.at[s], r3s.at[s], r3r.at[s]),
            Ring(xp, xm, take4, put4, r4.at[s], r4s.at[s], r4r.at[s]),
        )

    stages = [rings(0), rings(1)]

    def start(s):
        cot_copies[s].wait_recv()
        both = cot[:, :, 256 * s:256 * (s + 1)].reshape(2 * T, 256)
        coded_t[...] = jnp.transpose(both.astype(F32)).astype(BF16)
        ra, rb = stages[s][:2]
        top = lax.fori_loop(0, 4, product(s), jnp.zeros((1, 256), F32))
        ra.first(0)
        rb.first(0)
        top = lax.fori_loop(4, 8, product(s), top)
        ra.first(1)
        rb.first(1)
        return top

    def second(s, phase):
        ra, rb = stages[s][2 * phase:2 * phase + 2]
        for p in range(2):
            ra.second(p)
            rb.second(p)

    def turn(s):
        for p in range(2):
            for k in range(2):
                stages[s][k].finish(p)
                stages[s][2 + k].first(p)

    z_copies = {}

    def z_send(s):
        for p in range(2):
            for k in range(2):
                stages[s][2 + k].finish(p)
        for i in range(1, NZ):
            zd = lax.rem(z + i, NZ)
            copy = pltpu.make_async_remote_copy(
                src_ref=fin.at[s, zd], dst_ref=zrecv.at[s, i], send_sem=zs.at[s, i], recv_sem=zr.at[s, i],
                device_id=at(dz=i), device_id_type=MESH,
            )
            copy.start()
            z_copies[s, i] = copy

    c_copies = {}
    j = xhi * NY + y

    def c_send(s):
        total = fin[s, z].astype(F32)
        for i in range(1, NZ):
            z_copies[s, i].wait_recv()
            total += zrecv[s, i].astype(F32)
        piece[s] = total.astype(BF16)
        for i, (dx, dy) in enumerate(GROUP):
            copy = pltpu.make_async_remote_copy(
                src_ref=piece.at[s], dst_ref=piece_all.at[pl.ds(2 * s, 2), j], send_sem=cs.at[s, i],
                recv_sem=cr.at[s, i], device_id=at(dx=dx, dy=dy), device_id_type=MESH,
            )
            copy.start()
            c_copies[s, i] = copy
        piece_all[pl.ds(2 * s, 2), j] = piece[s]

    def own_out(f):
        return pltpu.make_async_copy(
            mine_v.at[f], grad_hbm.at[:, pl.ds(pl.multiple_of(f * 512 + c * 256, 256), 256)], own_o.at[f]
        )

    def mate_out(f):
        return pltpu.make_async_remote_copy(
            src_ref=other_v.at[f],
            dst_ref=grad_hbm.at[:, pl.ds(pl.multiple_of(f * 512 + c * 256, 256), 256)],
            send_sem=oth_s.at[f], recv_sem=oth_r.at[f], device_id=mate, device_id_type=MESH,
        )

    def input_grad(zb):
        zb = lax.rem(zb + NZ, NZ)

        def one(xl, _):
            f = zb * 2 + xl
            rows = cot[...].reshape(2 * T, KV)
            out = lax.dot_general(rows, wfull[f], (((1,), (1,)), ((), ())), preferred_element_type=F32)
            out = out.astype(BF16)
            mine_v[f] = out[0:T]
            other_v[f] = out[T:2 * T]
            own_out(f).start()
            mate_out(f).start()
            return 0

        lax.fori_loop(0, 2, one, 0)

    v_copies = []

    def v_send(s):
        for i in range(len(GROUP)):
            c_copies[s, i].wait_recv()
        cols = pl.ds(256 * s, 256)
        turned = jnp.transpose(piece_all[pl.ds(2 * s, 2)].reshape(256, 256).astype(F32))
        vout[:, 256 * s:256 * (s + 1)] = turned.astype(BF16)
        rows = pl.ds(pl.multiple_of(c * 256, 256), 256)
        own = pltpu.make_async_copy(vout.at[:, cols], value_hbm.at[rows, cols], v_o.at[s])
        own.start()
        copy = pltpu.make_async_remote_copy(
            src_ref=vout.at[:, cols], dst_ref=value_hbm.at[rows, cols], send_sem=v_s.at[s], recv_sem=v_r.at[s],
            device_id=mate, device_id_type=MESH,
        )
        copy.start()
        v_copies.extend([own, copy])

    across(0, own_rows, fsdp, (0, 128))
    az_send(1, 0)
    top_g = attention(0)
    top_g = jnp.maximum(top_g, attention(1))
    cot_send(0)
    top_g = jnp.maximum(top_g, attention(2))
    across_wait(0, 1)
    az_send(1, 1)
    top_x = start(0)
    top_g = jnp.maximum(top_g, attention(3))
    cot_send(1)
    second(0, 0)
    start(1)
    w_own.wait()
    top_w = jnp.max(jnp.abs(wfull[fsdp].astype(F32)), axis=0, keepdims=True)
    row = lax.broadcasted_iota(jnp.int32, (8, 128), 0)
    tops = [jnp.max(top, axis=1, keepdims=True) for top in (top_x, top_w, top_g)]
    pk[0] = jnp.where(row == 0, tops[0], jnp.where(row == 1, tops[1], tops[2]))
    peak_send(0, [at(dx=dx, dc=dc) for dx, dc in LINE], pk1, p1s, p1r)
    az_wait(1, 0)
    az_send(2, 0)
    turn(0)
    az_wait(1, 1)
    az_send(2, 1)
    across_wait(0, 0)
    input_grad(z)
    second(1, 0)
    second(0, 1)
    peak_join(0, len(LINE), pk1, p1r)
    peak_send(1, [at(dy=dy) for dy in range(1, NY)], pk2, p2s, p2r)
    az_wait(2, 0)
    az_send(3, 0)
    z_send(0)
    turn(1)
    az_wait(2, 1)
    az_send(3, 1)
    for dz in (1, -1, 2, -2):
        spread(dz)
    peak_join(1, NY - 1, pk2, p2r)
    peak_send(2, [at(dz=dz) for dz in range(1, NZ)], pk3, p3s, p3r)
    second(1, 1)
    c_send(0)
    z_send(1)
    az_wait(3, 0)
    az_send(4, 0)
    spread(3)
    spread(-3)
    for dz in (1, -1):
        across_wait(1 + dz % NZ, 0)
        input_grad(z + dz)
    peak_join(2, NZ - 1, pk3, p3r)
    peak_out[...] = pk[3]
    v_send(0)
    c_send(1)
    az_wait(3, 1)
    az_send(4, 1)
    az_wait(4, 0)
    spread(4)
    for dz in (2, -2, 3, -3):
        across_wait(1 + dz % NZ, 0)
        input_grad(z + dz)
    v_send(1)
    az_wait(4, 1)
    across_wait(1 + 4, 0)
    input_grad(z + 4)

    for copy in ax.values():
        copy.wait_send()
    for copy in az.values():
        copy.wait_send()
    for copy in pk_copies + cot_copies + list(z_copies.values()) + list(c_copies.values()):
        copy.wait_send()
    for ring in stages[0] + stages[1]:
        ring.drain()

    def last(f, _):
        x_swap(f).wait_send()
        own_out(f).wait()
        mate_out(f).wait()
        return 0

    lax.fori_loop(0, 16, last, 0)
    for copy in v_copies:
        copy.wait()


def hand_over(value, grad, peaks, value_out, grad_out, peaks_out, weight_out, value_v, grad_v, come, leave):
    parts = [(value, value_v, value_out)]
    for i in range(CUTS):
        cols = pl.ds(i * (D // CUTS), D // CUTS)
        parts.append((grad.at[:, cols], grad_v.at[:, cols], grad_out.at[:, cols]))
    arrive = [pltpu.make_async_copy(a, b, come.at[i]) for i, (a, b, _) in enumerate(parts)]
    depart = [pltpu.make_async_copy(b, a, leave.at[i]) for i, (_, b, a) in enumerate(parts)]
    for copy in arrive:
        copy.start()
    peaks_out[0] = peaks[0, 0]
    peaks_out[1] = peaks[2, 0]
    weight_out[0] = peaks[1, 0]
    for a, b in zip(arrive, depart):
        a.wait()
        b.start()
    for copy in depart:
        copy.wait()


def body(layer_input, queries, keys, context_gradient, weight):
    dma = pltpu.SemaphoreType.DMA
    vm = pltpu.VMEM
    anywhere = pl.BlockSpec(memory_space=pl.ANY)
    scalars = pl.BlockSpec(memory_space=pltpu.SMEM)
    value_grad, input_grad, peaks = pl.pallas_call(
        kernel,
        out_shape=(
            jax.ShapeDtypeStruct((512, KV), BF16),
            jax.ShapeDtypeStruct((T, D), BF16),
            jax.ShapeDtypeStruct((8, 128), F32),
        ),
        in_specs=[anywhere] * 5,
        out_specs=(anywhere, anywhere, pl.BlockSpec(memory_space=pltpu.VMEM)),
        scratch_shapes=[
            vm((16, 2 * T, 256), BF16), vm((T, 4096), BF16), vm((T, KV), BF16), vm((T, 4096), BF16),
            vm((16, 256, KV), BF16), vm((2, T, KV), BF16), vm((256, 2 * T), BF16),
            vm((2, NZ, 2, 2, 2, NY, 16, 256), BF16), vm((2, NZ, NY, 16, 256), BF16),
            vm((2, NZ, 2, 2, 16, 256), BF16), vm((2, NZ, 2, 16, 256), BF16),
            vm((2, 6, 4, NY, 16, 256), BF16), vm((2, 6, 4, 2, 2, 16, 256), BF16),
            vm((2, 6, 4, 16, 256), BF16), vm((2, 6, 4, 16, 256), BF16),
            vm((2, NZ, 2, 16, 256), BF16), vm((2, 2, 16, 256), BF16), vm((4, 8, 16, 256), BF16),
            vm((256, KV), BF16),
            vm((16, T, 256), BF16), vm((16, T, 256), BF16),
            vm((4, 8, 128), F32), vm((7, 8, 128), F32), vm((3, 8, 128), F32), vm((7, 8, 128), F32),
            dma((9,)), dma((16,)), dma((16,)), dma((16,)), dma, dma((36,)), dma((36,)), dma((16,)), dma((16,)),
            dma((2,)), dma((2,)), dma((7,)), dma((7,)), dma((3,)), dma((3,)), dma((7,)), dma((7,)),
            dma((2, 6)), dma((2, 6)), dma((2, 6)), dma((2, 6)), dma((2, 6)), dma((2, 6)), dma((2, 6)), dma((2, 6)),
            dma((2, 8)), dma((2, 8)), dma((2, 7)), dma((2, 7)), dma((16,)), dma((16,)), dma((16,)), dma((2,)), dma((2,)), dma((2,)),
        ],
        compiler_params=pltpu.CompilerParams(
            collective_id=0, has_side_effects=True, vmem_limit_bytes=60 << 20
        ),
        name="value_backward",
    )(layer_input, queries, keys, context_gradient, weight)
    return pl.pallas_call(
        hand_over,
        out_shape=(
            jax.ShapeDtypeStruct((512, KV), BF16),
            jax.ShapeDtypeStruct((T, D), BF16),
            jax.ShapeDtypeStruct((2,), F32),
            jax.ShapeDtypeStruct((1,), F32),
        ),
        in_specs=[anywhere, anywhere, scalars],
        out_specs=(anywhere, anywhere, scalars, scalars),
        scratch_shapes=[vm((512, KV), BF16), vm((T, D), BF16), dma((1 + CUTS,)), dma((1 + CUTS,))],
        compiler_params=pltpu.CompilerParams(vmem_limit_bytes=60 << 20),
        name="hand_over",
    )(value_grad, input_grad, peaks)


def solution(mesh):
    return jax.shard_map(
        body,
        mesh=mesh,
        in_specs=(
            P(("rep", "fsdp"), None),
            P(("rep", "fsdp"), None),
            P(("rep", "fsdp"), None),
            P(("rep", "fsdp"), None),
            P("fsdp", None),
        ),
        out_specs=(P("fsdp", None), P(("rep", "fsdp"), None), P(), P()),
        check_vma=False,
    )
```

time: 88 us -> 74.3 us (0.84)
  local copies, waits for them, and re-layouts: 7.04 us -> 0 us
  Pallas kernels: 78.3 us -> 73.5 us
  other arithmetic: 1.88 us -> 0 us
    pallas_call x1, Pallas kernels: 78.3 us -> 69.2 us  [body(): pl.pallas_call(kernel, out_shape=(jax.ShapeDtypeStruct((512, KV), BF16),...]
    unnamed x2 -> x0, local copies, waits for them, and re-layouts: 5.72 us -> none
    pallas_call x0 -> x1, Pallas kernels: none -> 4.29 us  [body(): pl.pallas_call(hand_over, out_shape=(jax.ShapeDtypeStruct((512, KV), BF16...]
    another operation x1 -> x0, other arithmetic: 1.88 us -> none  [body(): jnp.stack([peaks[0, 0], peaks[2, 0]])]
    slice x1 -> x0, local copies, waits for them, and re-layouts: 1.32 us -> none  [body(): peaks[1, 0:1]]
where the time goes in v2:
time: 74.3 us; the launch traced here: 74.1 us
  Pallas kernels  73.5 us (99%)
    pallas_call x1, Pallas kernels, body(): pl.pallas_call(kernel, out_shape=(jax.ShapeDtypeStruct((512, KV), BF16),...  69.2 us
    pallas_call x1, Pallas kernels, body(): pl.pallas_call(hand_over, out_shape=(jax.ShapeDtypeStruct((512, KV), BF16...  4.29 us

profile of v2, /device:TPU:1, one launch (start us, length us, event | category | flops | bytes accessed | tf_op | source)
XLA Modules:
  0.0 74.1 jit_solution(2891424085140741944)
XLA Ops:
  0.6 69.2 %value_backward.1 = (bf16[512,512]{1,0:T(8,128)(2,1)}, bf16[192,8192]{1,0:T(8,128)(2,1)}, f32[8,128]{1,0:T(8,128)}) custom-call(bf16[192,8192]{1,0:T(8,128)(2,1)} %x_hbm.1, bf16[192,4096]{1,0:T(8,128)(2,1)} %q_hbm.1, bf16[192,512]{1,0:T(8,128)(2,1)} %k_hbm.1, bf16[192,4096]{1,0:T(8,128)(2,1)} %g_hbm.1, bf16[512,512]{1,0:T(8,128)(2,1)} %w_hbm.1), custom_call_target="tpu_custom_call" | custom-call | tf_op jit(solution)/shard_map/value_backward/pallas_call | solution.py:536
  69.8 4.3 %hand_over.1 = (bf16[512,512]{1,0:T(8,128)(2,1)}, bf16[192,8192]{1,0:T(8,128)(2,1)}, f32[2]{0:T(128)}, f32[1]{0:T(128)}) custom-call(bf16[512,512]{1,0:T(8,128)(2,1)} %get-tuple-element.7.value, bf16[192,8192]{1,0:T(8,128)(2,1)} %get-tuple-element.8.grad, f32[8,128]{1,0:T(8,128)} %get-tuple-element.9.peaks), custom_call_target="tpu_custom_call" | custom-call | tf_op jit(solution)/shard_map/hand_over/pallas_call | solution.py:566

commit v3 on v2

v3 whole, which is shorter than its diff:
```python
import functools
import math

import jax
import jax.numpy as jnp
from jax import lax
from jax.experimental import pallas as pl
from jax.experimental.pallas import tpu as pltpu
from jax.sharding import PartitionSpec as P

HEAD = 128
QUERY_HEADS = 32
KV_HEADS = 4
PER_KV = QUERY_HEADS // KV_HEADS
T = 192
D = 8192
KV = KV_HEADS * HEAD
MESH = pl.DeviceIdType.MESH
F32 = jnp.float32
BF16 = jnp.bfloat16
NX, NY, NZ = 4, 4, 8
CUTS = 4


def place(x, y, z, c):
    x = lax.rem(x + NX, NX)
    y = lax.rem(y + NY, NY)
    z = lax.rem(z + NZ, NZ)
    c = lax.rem(c, 2)
    return ((y * 2 + x // 2) * 2 + c, z * 2 + lax.rem(x, 2))


class Straight:
    def __init__(self, targets, take, put, bufs, send, recv):
        self.targets, self.take, self.put = targets, take, put
        self.bufs, self.send, self.recv = bufs, send, recv

    def first(self, part):
        for i, to in enumerate(self.targets):
            copy = pltpu.make_async_remote_copy(
                src_ref=self.take(part, i + 1), dst_ref=self.bufs.at[part, i], send_sem=self.send,
                recv_sem=self.recv.at[part], device_id=to, device_id_type=MESH,
            )
            copy.start()

    def finish(self, part):
        landed(self.bufs.at[part], self.recv.at[part])
        mine = self.take(part, 0)

        def add(k, _):
            total = mine[k].astype(F32)
            for i in range(3):
                total += self.bufs[part, i, k].astype(F32)
            self.put(4 * part + k, total)
            return 0

        lax.fori_loop(0, 4, add, 0)

    def drain(self):
        landed(self.bufs, self.send)


LINE = [(dx, dc) for dx in range(NX) for dc in range(2) if (dx, dc) != (0, 0)]
GROUP = [(dx, dy) for dx in (0, 2) for dy in range(NY) if (dx, dy) != (0, 0)]
PARTNERS = sorted(
    set((dx, 0, 0, dc) for dx, dc in LINE)
    | set((0, dy, 0, 0) for dy in range(1, NY))
    | set((0, 0, dz, 0) for dz in range(1, NZ))
    | set((dx, dy, 0, 0) for dx, dy in GROUP)
)


def landed(view, sem):
    pltpu.make_async_copy(view, view, sem).wait()


class Ring:
    def __init__(self, plus, minus, take, put, bufs, send, recv):
        self.plus, self.minus, self.take, self.put = plus, minus, take, put
        self.bufs, self.send, self.recv = bufs, send, recv

    def go(self, src, slot, to):
        copy = pltpu.make_async_remote_copy(
            src_ref=src, dst_ref=self.bufs.at[slot], send_sem=self.send,
            recv_sem=self.recv.at[slot], device_id=to, device_id_type=MESH,
        )
        copy.start()

    def arrived(self, slot):
        landed(self.bufs.at[slot], self.recv.at[slot])

    def first(self, part):
        if part == 0:
            self.go(self.take(0, 2), 0, self.plus)
            self.go(self.take(0, -1), 2, self.minus)
        else:
            self.go(self.take(1, 2), 1, self.minus)
            self.go(self.take(1, 1), 3, self.plus)

    def second(self, part):
        step = 1 if part == 0 else -1
        self.arrived(part)
        mine = self.take(part, step)

        def add(i, _):
            mine[i] = (mine[i].astype(F32) + self.bufs[part, i].astype(F32)).astype(BF16)
            return 0

        lax.fori_loop(0, 4, add, 0)
        self.go(mine, 4 + part, self.plus if part == 0 else self.minus)

    def finish(self, part):
        self.arrived(2 + part)
        self.arrived(4 + part)
        mine = self.take(part, 0)

        def add(i, _):
            total = mine[i].astype(F32) + self.bufs[2 + part, i].astype(F32)
            self.put(4 * part + i, total + self.bufs[4 + part, i].astype(F32))
            return 0

        lax.fori_loop(0, 4, add, 0)

    def drain(self):
        landed(self.bufs, self.send)


def kernel(
    x_hbm, q_hbm, k_hbm, g_hbm, w_hbm,
    value_v, grad_v, peak_out,
    xh, q_v, k_v, g_v, wfull, cot, coded_t,
    part_v, xbuf, ybuf, fin, r1, r2, r3, r4, zrecv, piece, piece_all,
    other_v, pk, pk1, pk2, pk3, x_out,
    load_sem, xown_sem, xother_sem, xs_sem, xr_sem, wown_sem, ax_s, ax_r, az_s, az_r,
    cot_s, cot_r, p1s, p1r, p2s, p2r, p3s, p3r,
    r1s, r1r, r2s, r2r, r3s, r3r, r4s, r4r, zs, zr, cs, cr, oth_s, oth_r, v_s, v_r,
):
    rep, fsdp = lax.axis_index("rep"), lax.axis_index("fsdp")
    c = lax.rem(rep, 2)
    xhi = lax.rem(rep // 2, 2)
    y = rep // 4
    xlo = lax.rem(fsdp, 2)
    z = fsdp // 2
    x = 2 * xhi + xlo
    xot = 1 - xlo

    def at(dx=0, dy=0, dz=0, dc=0):
        return place(x + dx, y + dy, z + dz, c + dc)

    mate = at(dc=1)
    barrier = pltpu.get_barrier_semaphore()
    for partner in PARTNERS:
        pl.semaphore_signal(barrier, inc=1, device_id=at(*partner), device_id_type=MESH)

    def half_cols(f, half):
        return x_hbm.at[:, pl.ds(pl.multiple_of(f * 512 + half * 256, 256), 256)]

    def x_own(f):
        return pltpu.make_async_copy(half_cols(f, c), xh.at[f, pl.ds(0, T), :], xown_sem)

    def x_other(f):
        return pltpu.make_async_copy(half_cols(f, 1 - c), x_out.at[f], xother_sem)

    def x_swap(f):
        return pltpu.make_async_remote_copy(
            src_ref=x_out.at[f], dst_ref=xh.at[f, pl.ds(T, T), :], send_sem=xs_sem,
            recv_sem=xr_sem.at[f // 8], device_id=mate, device_id_type=MESH,
        )

    def x_give(f, _):
        x_swap(f).start()
        return 0


    lax.fori_loop(0, 16, lambda f, _: (x_other(f).start(), 0)[1], 0)
    loads = [pltpu.make_async_copy(k_hbm, k_v, load_sem.at[4])]
    for a in range(KV_HEADS):
        cols = pl.ds(a * PER_KV * HEAD, PER_KV * HEAD)
        loads.append(pltpu.make_async_copy(q_hbm.at[:, cols], q_v.at[:, cols], load_sem.at[a]))
        loads.append(pltpu.make_async_copy(g_hbm.at[:, cols], g_v.at[:, cols], load_sem.at[a]))
    w_half = w_hbm.at[pl.ds(pl.multiple_of(c * 256, 256), 256), :]
    w_own = pltpu.make_async_copy(w_half, wfull.at[fsdp], wown_sem)
    for copy in loads[:5]:
        copy.start()
    w_own.start()
    lax.fori_loop(0, 16, lambda f, _: (x_own(f).start(), 0)[1], 0)
    for copy in loads[5:]:
        copy.start()

    key_pos = lax.broadcasted_iota(jnp.int32, (T, 2 * T), 0)
    query_pos = lax.broadcasted_iota(jnp.int32, (T, 2 * T), 1)
    keep = key_pos <= jnp.where(query_pos >= T, query_pos - T, query_pos)

    def attention(a):
        if a == 0:
            loads[0].wait()
        landed(q_v.at[:, pl.ds(0, 2 * PER_KV * HEAD)], load_sem.at[a])
        keys = k_v[:, a * HEAD:(a + 1) * HEAD]
        total = jnp.zeros((T, HEAD), F32)
        for pair in range(PER_KV // 2):
            base = (a * PER_KV + 2 * pair) * HEAD
            qs = jnp.concatenate([q_v[:, base:base + HEAD], q_v[:, base + HEAD:base + 2 * HEAD]], axis=0)
            gs = jnp.concatenate([g_v[:, base:base + HEAD], g_v[:, base + HEAD:base + 2 * HEAD]], axis=0)
            scores = lax.dot_general(
                keys, qs, (((1,), (1,)), ((), ())), preferred_element_type=F32
            ) * (1.0 / math.sqrt(HEAD))
            scores = jnp.where(keep, scores, -jnp.inf)
            expo = jnp.exp(scores - jnp.max(scores, axis=0, keepdims=True))
            prob = (expo * (1.0 / jnp.sum(expo, axis=0, keepdims=True))).astype(BF16)
            total += jnp.dot(prob, gs, preferred_element_type=F32)
        cot[0, :, a * HEAD:(a + 1) * HEAD] = total.astype(BF16)
        return jnp.max(jnp.abs(total), axis=0, keepdims=True)

    top_g = attention(0)
    pl.semaphore_wait(barrier, len(PARTNERS))
    landed(x_out, xother_sem)
    lax.fori_loop(0, 16, x_give, 0)

    def across(b, src, block, rows):
        for i, dx in enumerate((1, -1)):
            for k, base in enumerate(rows):
                part = pl.ds(base + 64 * i, 64)
                copy = pltpu.make_async_remote_copy(
                    src_ref=src(base + 64 * i), dst_ref=wfull.at[block, part, :],
                    send_sem=ax_s.at[b + 8 * k], recv_sem=ax_r.at[b + 8 * k], device_id=at(dx=dx), device_id_type=MESH,
                )
                copy.start()

    def across_wait(b, k):
        landed(wfull.at[0, pl.ds(0, 128), :], ax_r.at[b + 8 * k])

    def own_rows(base):
        return wfull.at[fsdp, pl.ds(base, 64), :]

    def spread(dz):
        block = lax.rem(z + dz + NZ, NZ) * 2 + xlo
        across(dz % NZ, lambda base: wfull.at[block, pl.ds(base, 64), :], block, (0,))

    WHOLE, LATE, FIRST, LAST = (0, 256), (128, 128), (0, 192), (192, 64)

    def az_list(d, p):
        if d < 4:
            return [(way, 0, WHOLE if p == 0 else LATE) for way in range(2)]
        return [(0, 0, FIRST), (1, 0, LAST)] if p == 0 else [(1, 0, LATE)]

    def az_slot(d, p):
        return (d - 1) * 2 + p

    def az_view(d, p):
        if p == 0 and d < 4:
            return wfull.at[pl.ds(0, 2)]
        return wfull.at[0, pl.ds(0, 128 if p == 1 and d == 4 else 256), :]

    def az_send(d, p):
        for way, _, (base, count) in az_list(d, p):
            dz = 1 - 2 * way
            block = lax.rem(z - dz * (d - 1) + NZ, NZ) * 2 + (xlo if p == 0 else xot)
            slot = az_slot(d, p)
            rows = pl.ds(base, count)
            copy = pltpu.make_async_remote_copy(
                src_ref=wfull.at[block, rows, :], dst_ref=wfull.at[block, rows, :], send_sem=az_s.at[slot], recv_sem=az_r.at[slot],
                device_id=at(dz=dz), device_id_type=MESH,
            )
            copy.start()

    def az_wait(d, p):
        landed(az_view(d, p), az_r.at[az_slot(d, p)])

    cot_copies = []

    def cot_send(s):
        cols = pl.ds(256 * s, 256)
        cot_copies.append(pltpu.make_async_remote_copy(
            src_ref=cot.at[0, :, cols], dst_ref=cot.at[1, :, cols], send_sem=cot_s.at[s], recv_sem=cot_r.at[s],
            device_id=mate, device_id_type=MESH,
        ))
        cot_copies[-1].start()

    def peak_send(stage, targets, got, s_sem, r_sem):
        for i, to in enumerate(targets):
            copy = pltpu.make_async_remote_copy(
                src_ref=pk.at[stage], dst_ref=got.at[i], send_sem=s_sem, recv_sem=r_sem,
                device_id=to, device_id_type=MESH,
            )
            copy.start()

    def peak_join(stage, count, got, r_sem):
        top = pk[stage]
        landed(got, r_sem)
        for i in range(count):
            top = jnp.maximum(top, got[i])
        pk[stage + 1] = top

    def product(s):
        def one(pair, _):
            for k in range(4):
                zd, xl = pair * 2 + k // 2, k % 2
                out = jnp.dot(coded_t[...], xh[zd * 2 + xl], preferred_element_type=F32)
                part_v[s, zd, xl] = out.astype(BF16).reshape(2, 2, NY, 16, 256)
            return 0
        return one

    def xdest(step):
        xd = lax.rem(x + step + NX, NX)
        return lax.rem(xd, 2), xd // 2

    def ydest(step):
        return lax.rem(y + step + NY, NY)

    xp, xm, yp, ym = at(dx=1), at(dx=-1), at(dy=1), at(dy=-1)

    def rings(s):
        def take1(p, step):
            xl, xg = xdest(step)
            return part_v.at[s, pl.ds(4 * p, 4), xl, 0, xg]

        def take2(p, step):
            return part_v.at[s, pl.ds(4 * p, 4), :, 1, :, ydest(step)]

        def take3(p, step):
            return xbuf.at[s, pl.ds(4 * p, 4), ydest(step)]

        def take4(p, step):
            xl, xg = xdest(step)
            return ybuf.at[s, pl.ds(4 * p, 4), xl, xg]

        def put1(i, v):
            xbuf[s, i] = v.astype(BF16)

        def put2(i, v):
            ybuf[s, i] = v.astype(BF16)

        def put3(i, v):
            fin[s, i, 0] = v.astype(BF16)

        def put4(i, v):
            fin[s, i, 1] = v.astype(BF16)

        return (
            Ring(xp, xm, take1, put1, r1.at[s], r1s.at[s], r1r.at[s]),
            Ring(yp, ym, take2, put2, r2.at[s], r2s.at[s], r2r.at[s]),
            Straight([at(dy=i) for i in (1, 2, 3)], take3, put3, r3.at[s], r3s.at[s], r3r.at[s]),
            Straight([at(dx=i) for i in (1, 2, 3)], take4, put4, r4.at[s], r4s.at[s], r4r.at[s]),
        )

    stages = [rings(0), rings(1)]

    def start(s):
        cot_copies[s].wait_recv()
        both = cot[:, :, 256 * s:256 * (s + 1)].reshape(2 * T, 256)
        coded_t[...] = jnp.transpose(both.astype(F32)).astype(BF16)
        ra, rb = stages[s][:2]
        if s == 0:
            landed(x_out, xown_sem)
            landed(x_out.at[pl.ds(0, 8)], xr_sem.at[0])
        lax.fori_loop(0, 2, product(s), 0)
        ra.first(0)
        rb.first(0)
        if s == 0:
            landed(x_out.at[pl.ds(0, 8)], xr_sem.at[1])
        lax.fori_loop(2, 4, product(s), 0)
        ra.first(1)
        rb.first(1)

    def second(s):
        ra, rb = stages[s][:2]
        for p in range(2):
            ra.second(p)
            rb.second(p)

    def turn(s):
        for p in range(2):
            for k in range(2):
                stages[s][k].finish(p)
                stages[s][2 + k].first(p)

    def z_send(s):
        for p in range(2):
            for k in range(2):
                stages[s][2 + k].finish(p)
        for i in range(1, NZ):
            zd = lax.rem(z + i, NZ)
            copy = pltpu.make_async_remote_copy(
                src_ref=fin.at[s, zd], dst_ref=zrecv.at[s, i], send_sem=zs.at[s], recv_sem=zr.at[s],
                device_id=at(dz=i), device_id_type=MESH,
            )
            copy.start()

    j = xhi * NY + y

    def c_send(s):
        total = fin[s, z].astype(F32)
        landed(zrecv.at[s, pl.ds(1, NZ - 1)], zr.at[s])
        for i in range(1, NZ):
            total += zrecv[s, i].astype(F32)
        piece[s] = (total * (1.0 / 256.0)).astype(BF16)
        for i, (dx, dy) in enumerate(GROUP):
            copy = pltpu.make_async_remote_copy(
                src_ref=piece.at[s], dst_ref=piece_all.at[pl.ds(2 * s, 2), j], send_sem=cs.at[s],
                recv_sem=cr.at[s], device_id=at(dx=dx, dy=dy), device_id_type=MESH,
            )
            copy.start()
        piece_all[pl.ds(2 * s, 2), j] = piece[s]

    def out_cols(f):
        return pl.ds(pl.multiple_of(f * 512 + c * 256, 256), 256)

    def mate_out(f):
        return pltpu.make_async_remote_copy(
            src_ref=other_v.at[f], dst_ref=grad_v.at[:, out_cols(f)],
            send_sem=oth_s, recv_sem=oth_r, device_id=mate, device_id_type=MESH,
        )

    def input_grad(zb):
        zb = lax.rem(zb + NZ, NZ)

        rows = cot[...].reshape(2 * T, KV)
        for xl in range(2):
            f = zb * 2 + xl
            out = lax.dot_general(rows, wfull[f], (((1,), (1,)), ((), ())), preferred_element_type=F32)
            out = out.astype(BF16)
            grad_v[:, out_cols(f)] = out[0:T]
            other_v[f] = out[T:2 * T]
        for xl in range(2):
            mate_out(zb * 2 + xl).start()

    v_copies = []

    def v_send(s):
        landed(zrecv.at[s, pl.ds(1, NZ - 1)], cr.at[s])
        cols = pl.ds(256 * s, 256)
        turned = jnp.transpose(piece_all[pl.ds(2 * s, 2)].reshape(256, 256).astype(F32))
        rows = pl.ds(pl.multiple_of(c * 256, 256), 256)
        value_v[rows, cols] = turned.astype(BF16)
        copy = pltpu.make_async_remote_copy(
            src_ref=value_v.at[rows, cols], dst_ref=value_v.at[rows, cols], send_sem=v_s.at[s], recv_sem=v_r.at[s],
            device_id=mate, device_id_type=MESH,
        )
        copy.start()
        v_copies.append(copy)

    w_own.wait()
    across(0, own_rows, fsdp, (0, 128))
    az_send(1, 0)
    top_g = jnp.maximum(top_g, attention(1))
    cot_send(0)
    top_g = jnp.maximum(top_g, attention(2))
    top_g = jnp.maximum(top_g, attention(3))
    cot_send(1)
    start(0)
    across_wait(0, 1)
    az_send(1, 1)
    start(1)
    second(0)
    az_wait(1, 0)
    az_send(2, 0)
    top_x = lax.fori_loop(
        0, 16,
        lambda f, top: jnp.maximum(top, jnp.max(jnp.abs(xh[f].astype(F32)), axis=0, keepdims=True)),
        jnp.zeros((1, 256), F32),
    )
    top_w = jnp.max(jnp.abs(wfull[fsdp].astype(F32)), axis=0, keepdims=True)
    row = lax.broadcasted_iota(jnp.int32, (8, 128), 0)
    tops = [jnp.max(top, axis=1, keepdims=True) for top in (top_x, top_w, top_g)]
    pk[0] = jnp.where(row == 0, tops[0], jnp.where(row == 1, tops[1], tops[2]))
    peak_send(0, [at(dx=dx, dc=dc) for dx, dc in LINE], pk1, p1s, p1r)
    second(1)
    az_wait(1, 1)
    az_send(2, 1)
    turn(0)
    across_wait(0, 0)
    input_grad(z)
    az_wait(2, 0)
    az_send(3, 0)
    turn(1)
    spread(1)
    spread(-1)
    peak_join(0, len(LINE), pk1, p1r)
    peak_send(1, [at(dy=dy) for dy in range(1, NY)], pk2, p2s, p2r)
    az_wait(2, 1)
    az_send(3, 1)
    z_send(0)
    z_send(1)
    spread(2)
    spread(-2)
    az_wait(3, 0)
    az_send(4, 0)
    for dz in (1, -1):
        across_wait(dz % NZ, 0)
        input_grad(z + dz)
    c_send(0)
    az_wait(3, 1)
    az_send(4, 1)
    spread(3)
    spread(-3)
    peak_join(1, NY - 1, pk2, p2r)
    peak_send(2, [at(dz=dz) for dz in range(1, NZ)], pk3, p3s, p3r)
    c_send(1)
    for dz in (2, -2):
        across_wait(dz % NZ, 0)
        input_grad(z + dz)
    az_wait(4, 0)
    spread(4)
    v_send(0)
    for dz in (3, -3):
        across_wait(dz % NZ, 0)
        input_grad(z + dz)
    v_send(1)
    peak_join(2, NZ - 1, pk3, p3r)
    peak_out[...] = pk[3]
    az_wait(4, 1)
    across_wait(4, 0)
    input_grad(z + 4)

    for b in range(9):
        landed(wfull.at[0, pl.ds(0, 128), :], ax_s.at[b])
    for d in range(1, 5):
        for p in range(2):
            landed(az_view(d, p), az_s.at[az_slot(d, p)])
    for got, sem in ((pk1, p1s), (pk2, p2s), (pk3, p3s)):
        landed(got, sem)
    for s in range(2):
        cot_copies[s].wait_send()
        landed(zrecv.at[s, pl.ds(1, NZ - 1)], zs.at[s])
        landed(zrecv.at[s, pl.ds(1, NZ - 1)], cs.at[s])
    for ring in stages[0] + stages[1]:
        ring.drain()

    landed(x_out, xs_sem)
    landed(other_v, oth_s)
    landed(other_v, oth_r)
    for copy in v_copies:
        copy.wait()


def hand_over(value, grad, peaks, value_out, grad_out, peaks_out, weight_out, sems):
    copies = [pltpu.make_async_copy(value, value_out, sems.at[0])]
    for i in range(CUTS):
        rows = pl.ds(i * (T // CUTS), T // CUTS)
        copies.append(pltpu.make_async_copy(grad.at[rows], grad_out.at[rows], sems.at[1 + i]))
    for copy in copies:
        copy.start()
    peaks_out[0] = jnp.max(peaks[0:1])
    peaks_out[1] = jnp.max(peaks[2:3])
    weight_out[0] = jnp.max(peaks[1:2])
    for copy in copies:
        copy.wait()


def body(layer_input, queries, keys, context_gradient, weight):
    dma = pltpu.SemaphoreType.DMA
    vm = pltpu.VMEM
    anywhere = pl.BlockSpec(memory_space=pl.ANY)
    scalars = pl.BlockSpec(memory_space=pltpu.SMEM)
    value_grad, input_grad, peaks = pl.pallas_call(
        kernel,
        out_shape=(
            vm((512, KV), BF16),
            vm((T, D), BF16),
            vm((8, 128), F32),
        ),
        in_specs=[anywhere] * 5,
        out_specs=(pl.BlockSpec(memory_space=pltpu.VMEM),) * 3,
        scratch_shapes=[
            vm((16, 2 * T, 256), BF16), vm((T, 4096), BF16), vm((T, KV), BF16), vm((T, 4096), BF16),
            vm((16, 256, KV), BF16), vm((2, T, KV), BF16), vm((256, 2 * T), BF16),
            vm((2, NZ, 2, 2, 2, NY, 16, 256), BF16), vm((2, NZ, NY, 16, 256), BF16),
            vm((2, NZ, 2, 2, 16, 256), BF16), vm((2, NZ, 2, 16, 256), BF16),
            vm((2, 6, 4, NY, 16, 256), BF16), vm((2, 6, 4, 2, 2, 16, 256), BF16),
            vm((2, 2, 3, 4, 16, 256), BF16), vm((2, 2, 3, 4, 16, 256), BF16),
            vm((2, NZ, 2, 16, 256), BF16), vm((2, 2, 16, 256), BF16), vm((4, 8, 16, 256), BF16),
            vm((16, T, 256), BF16),
            vm((4, 8, 128), F32), vm((7, 8, 128), F32), vm((3, 8, 128), F32), vm((7, 8, 128), F32),
            vm((16, T, 256), BF16),
            dma((5,)), dma, dma, dma, dma((2,)), dma, dma((9,)), dma((9,)), dma((8,)), dma((8,)),
            dma((2,)), dma((2,)), dma, dma, dma, dma, dma, dma,
            dma((2,)), dma((2, 6)), dma((2,)), dma((2, 6)), dma((2,)), dma((2, 2)), dma((2,)), dma((2, 2)),
            dma((2,)), dma((2,)), dma((2,)), dma((2,)), dma, dma, dma((2,)), dma((2,)),
        ],
        compiler_params=pltpu.CompilerParams(
            collective_id=0, has_side_effects=True, vmem_limit_bytes=60 << 20
        ),
        name="value_backward",
    )(layer_input, queries, keys, context_gradient, weight)
    return pl.pallas_call(
        hand_over,
        out_shape=(
            jax.ShapeDtypeStruct((512, KV), BF16),
            jax.ShapeDtypeStruct((T, D), BF16),
            jax.ShapeDtypeStruct((2,), F32),
            jax.ShapeDtypeStruct((1,), F32),
        ),
        in_specs=[pl.BlockSpec(memory_space=pltpu.VMEM)] * 3,
        out_specs=(anywhere, anywhere, scalars, scalars),
        scratch_shapes=[dma((1 + CUTS,))],
        compiler_params=pltpu.CompilerParams(vmem_limit_bytes=1 << 20),
        name="hand_over",
    )(value_grad, input_grad, peaks)


def solution(mesh):
    return jax.shard_map(
        body,
        mesh=mesh,
        in_specs=(
            P(("rep", "fsdp"), None),
            P(("rep", "fsdp"), None),
            P(("rep", "fsdp"), None),
            P(("rep", "fsdp"), None),
            P("fsdp", None),
        ),
        out_specs=(P("fsdp", None), P(("rep", "fsdp"), None), P(), P()),
        check_vma=False,
    )
```

time: 74.3 us -> 63.8 us (0.86)
  Pallas kernels: 73.5 us -> 63.1 us
    pallas_call x1, Pallas kernels: 69.2 us -> 60.7 us  [body(): pl.pallas_call(kernel, out_shape=(vm((512, KV), BF16), vm((T, D), BF16),...]
    pallas_call x1, Pallas kernels: 4.29 us -> 2.4 us  [body(): pl.pallas_call(hand_over, out_shape=(jax.ShapeDtypeStruct((512, KV), BF16...]
where the time goes in v3:
time: 63.8 us
  Pallas kernels  63.1 us (99%)
  between operations  0.64 us (1%)
    pallas_call x1, Pallas kernels, body(): pl.pallas_call(kernel, out_shape=(vm((512, KV), BF16), vm((T, D), BF16),...  60.7 us
    pallas_call x1, Pallas kernels, body(): pl.pallas_call(hand_over, out_shape=(jax.ShapeDtypeStruct((512, KV), BF16...  2.4 us

profile of v3, /device:TPU:1, one launch (start us, length us, event | category | flops | bytes accessed | tf_op | source)
XLA Modules:
  0.0 63.8 jit_solution(9281939552761513155)
XLA Ops:
  0.6 60.7 %value_backward.1 = (bf16[512,512]{1,0:T(8,128)(2,1)S(1)}, bf16[192,8192]{1,0:T(8,128)(2,1)S(1)}, f32[8,128]{1,0:T(8,128)S(1)}) custom-call(bf16[192,8192]{1,0:T(8,128)(2,1)} %x_hbm.1, bf16[192,4096]{1,0:T(8,128)(2,1)} %q_hbm.1, bf16[192,512]{1,0:T(8,128)(2,1)} %k_hbm.1, bf16[192,4096]{1,0:T(8,128)(2,1)} %g_hbm.1, bf16[512,512]{1,0:T(8,128)(2,1)} %w_hbm.1), custom_call_target="tpu_custom_call" | custom-call | tf_op jit(solution)/shard_map/value_backward/pallas_call | solution.py:555
  61.4 2.4 %hand_over.1 = (bf16[512,512]{1,0:T(8,128)(2,1)}, bf16[192,8192]{1,0:T(8,128)(2,1)}, f32[2]{0:T(128)}, f32[1]{0:T(128)}) custom-call(bf16[512,512]{1,0:T(8,128)(2,1)S(1)} %get-tuple-element.7.value, bf16[192,8192]{1,0:T(8,128)(2,1)S(1)} %get-tuple-element.8.grad, f32[8,128]{1,0:T(8,128)S(1)} %get-tuple-element.9.peaks), custom_call_target="tpu_custom_call" | custom-call | tf_op jit(solution)/shard_map/hand_over/pallas_call | solution.py:585

commit v4 on v3

--- a/solution.py
+++ b/solution.py
@@ -20,6 +20,8 @@
 BF16 = jnp.bfloat16
 NX, NY, NZ = 4, 4, 8
 CUTS = 4
+EARLY = 128
+REST = 256 - EARLY
 
 
 def place(x, y, z, c):
@@ -36,10 +38,10 @@
         self.bufs, self.send, self.recv = bufs, send, recv
 
     def first(self, part):
-        for i, to in enumerate(self.targets):
+        for i in (1, 0, 2):
             copy = pltpu.make_async_remote_copy(
                 src_ref=self.take(part, i + 1), dst_ref=self.bufs.at[part, i], send_sem=self.send,
-                recv_sem=self.recv.at[part], device_id=to, device_id_type=MESH,
+                recv_sem=self.recv.at[part], device_id=self.targets[i], device_id_type=MESH,
             )
             copy.start()
 
@@ -61,12 +63,12 @@
 
 
 LINE = [(dx, dc) for dx in range(NX) for dc in range(2) if (dx, dc) != (0, 0)]
-GROUP = [(dx, dy) for dx in (0, 2) for dy in range(NY) if (dx, dy) != (0, 0)]
+GROUP = [(dx, dy, dc) for dx in (2, 0) for dy in (2, 1, 3, 0) for dc in (1, 0) if (dx, dy, dc) != (0, 0, 0)]
 PARTNERS = sorted(
     set((dx, 0, 0, dc) for dx, dc in LINE)
     | set((0, dy, 0, 0) for dy in range(1, NY))
     | set((0, 0, dz, 0) for dz in range(1, NZ))
-    | set((dx, dy, 0, 0) for dx, dy in GROUP)
+    | set((dx, dy, 0, dc) for dx, dy, dc in GROUP)
 )
 
 
@@ -129,11 +131,11 @@
     x_hbm, q_hbm, k_hbm, g_hbm, w_hbm,
     value_v, grad_v, peak_out,
     xh, q_v, k_v, g_v, wfull, cot, coded_t,
-    part_v, xbuf, ybuf, fin, r1, r2, r3, r4, zrecv, piece, piece_all,
+    part_x, part_y, xbuf, ybuf, fin, r1, r2, r3, r4, zrecv, piece, piece_all,
     other_v, pk, pk1, pk2, pk3, x_out,
     load_sem, xown_sem, xother_sem, xs_sem, xr_sem, wown_sem, ax_s, ax_r, az_s, az_r,
     cot_s, cot_r, p1s, p1r, p2s, p2r, p3s, p3r,
-    r1s, r1r, r2s, r2r, r3s, r3r, r4s, r4r, zs, zr, cs, cr, oth_s, oth_r, v_s, v_r,
+    r1s, r1r, r2s, r2r, r3s, r3r, r4s, r4r, zs, zr, cs, cr, oth_s, oth_r,
 ):
     rep, fsdp = lax.axis_index("rep"), lax.axis_index("fsdp")
     c = lax.rem(rep, 2)
@@ -216,32 +218,27 @@
     landed(x_out, xother_sem)
     lax.fori_loop(0, 16, x_give, 0)
 
-    def across(b, src, block, rows):
+    def across(b, block, base, count, sem):
         for i, dx in enumerate((1, -1)):
-            for k, base in enumerate(rows):
-                part = pl.ds(base + 64 * i, 64)
-                copy = pltpu.make_async_remote_copy(
-                    src_ref=src(base + 64 * i), dst_ref=wfull.at[block, part, :],
-                    send_sem=ax_s.at[b + 8 * k], recv_sem=ax_r.at[b + 8 * k], device_id=at(dx=dx), device_id_type=MESH,
-                )
-                copy.start()
+            view = wfull.at[block, pl.ds(base + i * (count // 2), count // 2), :]
+            copy = pltpu.make_async_remote_copy(
+                src_ref=view, dst_ref=view, send_sem=ax_s.at[sem], recv_sem=ax_r.at[sem],
+                device_id=at(dx=dx), device_id_type=MESH,
+            )
+            copy.start()
 
     def across_wait(b, k):
-        landed(wfull.at[0, pl.ds(0, 128), :], ax_r.at[b + 8 * k])
-
-    def own_rows(base):
-        return wfull.at[fsdp, pl.ds(base, 64), :]
+        landed(wfull.at[0, pl.ds(0, REST if k else EARLY), :], ax_r.at[8 if k else b])
 
     def spread(dz):
-        block = lax.rem(z + dz + NZ, NZ) * 2 + xlo
-        across(dz % NZ, lambda base: wfull.at[block, pl.ds(base, 64), :], block, (0,))
-
-    WHOLE, LATE, FIRST, LAST = (0, 256), (128, 128), (0, 192), (192, 64)
+        across(dz % NZ, lax.rem(z + dz + NZ, NZ) * 2 + xlo, 0, EARLY, dz % NZ)
+
+    WHOLE, LATE = (0, 256), (EARLY, REST)
 
     def az_list(d, p):
         if d < 4:
-            return [(way, 0, WHOLE if p == 0 else LATE) for way in range(2)]
-        return [(0, 0, FIRST), (1, 0, LAST)] if p == 0 else [(1, 0, LATE)]
+            return [(way, WHOLE if p == 0 else LATE) for way in range(2)]
+        return [(p, WHOLE)]
 
     def az_slot(d, p):
         return (d - 1) * 2 + p
@@ -249,10 +246,12 @@
     def az_view(d, p):
         if p == 0 and d < 4:
             return wfull.at[pl.ds(0, 2)]
-        return wfull.at[0, pl.ds(0, 128 if p == 1 and d == 4 else 256), :]
+        if p == 1 and d < 4:
+            return wfull.at[pl.ds(0, 2), pl.ds(0, REST), :]
+        return wfull.at[0]
 
     def az_send(d, p):
-        for way, _, (base, count) in az_list(d, p):
+        for way, (base, count) in az_list(d, p):
             dz = 1 - 2 * way
             block = lax.rem(z - dz * (d - 1) + NZ, NZ) * 2 + (xlo if p == 0 else xot)
             slot = az_slot(d, p)
@@ -296,7 +295,10 @@
             for k in range(4):
                 zd, xl = pair * 2 + k // 2, k % 2
                 out = jnp.dot(coded_t[...], xh[zd * 2 + xl], preferred_element_type=F32)
-                part_v[s, zd, xl] = out.astype(BF16).reshape(2, 2, NY, 16, 256)
+                out = out.astype(BF16).reshape(2, 2, NY, 16, 256)
+                part_x[s, xl, :, zd] = out[0]
+                for yd in range(NY):
+                    part_y[s, yd, zd, xl] = out[1, :, yd]
             return 0
         return one
 
@@ -312,23 +314,23 @@
     def rings(s):
         def take1(p, step):
             xl, xg = xdest(step)
-            return part_v.at[s, pl.ds(4 * p, 4), xl, 0, xg]
+            return part_x.at[s, xl, xg, pl.ds(4 * p, 4)]
 
         def take2(p, step):
-            return part_v.at[s, pl.ds(4 * p, 4), :, 1, :, ydest(step)]
+            return part_y.at[s, ydest(step), pl.ds(4 * p, 4)]
 
         def take3(p, step):
-            return xbuf.at[s, pl.ds(4 * p, 4), ydest(step)]
+            return xbuf.at[s, ydest(step), pl.ds(4 * p, 4)]
 
         def take4(p, step):
             xl, xg = xdest(step)
-            return ybuf.at[s, pl.ds(4 * p, 4), xl, xg]
+            return ybuf.at[s, xl, xg, pl.ds(4 * p, 4)]
 
         def put1(i, v):
-            xbuf[s, i] = v.astype(BF16)
+            xbuf[s, :, i] = v.astype(BF16)
 
         def put2(i, v):
-            ybuf[s, i] = v.astype(BF16)
+            ybuf[s, :, :, i] = v.astype(BF16)
 
         def put3(i, v):
             fin[s, i, 0] = v.astype(BF16)
@@ -378,7 +380,7 @@
         for p in range(2):
             for k in range(2):
                 stages[s][2 + k].finish(p)
-        for i in range(1, NZ):
+        for i in (4, 3, 5, 2, 6, 1, 7):
             zd = lax.rem(z + i, NZ)
             copy = pltpu.make_async_remote_copy(
                 src_ref=fin.at[s, zd], dst_ref=zrecv.at[s, i], send_sem=zs.at[s], recv_sem=zr.at[s],
@@ -394,13 +396,13 @@
         for i in range(1, NZ):
             total += zrecv[s, i].astype(F32)
         piece[s] = (total * (1.0 / 256.0)).astype(BF16)
-        for i, (dx, dy) in enumerate(GROUP):
+        for dx, dy, dc in GROUP:
             copy = pltpu.make_async_remote_copy(
-                src_ref=piece.at[s], dst_ref=piece_all.at[pl.ds(2 * s, 2), j], send_sem=cs.at[s],
-                recv_sem=cr.at[s], device_id=at(dx=dx, dy=dy), device_id_type=MESH,
+                src_ref=piece.at[s], dst_ref=piece_all.at[c, pl.ds(2 * s, 2), j], send_sem=cs.at[s],
+                recv_sem=cr.at[s], device_id=at(dx=dx, dy=dy, dc=dc), device_id_type=MESH,
             )
             copy.start()
-        piece_all[pl.ds(2 * s, 2), j] = piece[s]
+        piece_all[c, pl.ds(2 * s, 2), j] = piece[s]
 
     def out_cols(f):
         return pl.ds(pl.multiple_of(f * 512 + c * 256, 256), 256)
@@ -424,23 +426,24 @@
         for xl in range(2):
             mate_out(zb * 2 + xl).start()
 
-    v_copies = []
-
-    def v_send(s):
-        landed(zrecv.at[s, pl.ds(1, NZ - 1)], cr.at[s])
-        cols = pl.ds(256 * s, 256)
-        turned = jnp.transpose(piece_all[pl.ds(2 * s, 2)].reshape(256, 256).astype(F32))
-        rows = pl.ds(pl.multiple_of(c * 256, 256), 256)
-        value_v[rows, cols] = turned.astype(BF16)
-        copy = pltpu.make_async_remote_copy(
-            src_ref=value_v.at[rows, cols], dst_ref=value_v.at[rows, cols], send_sem=v_s.at[s], recv_sem=v_r.at[s],
-            device_id=mate, device_id_type=MESH,
-        )
-        copy.start()
-        v_copies.append(copy)
+    def c_view():
+        return wfull.at[0, pl.ds(0, 16 * len(GROUP)), :]
+
+    def v_turn(s):
+        landed(c_view(), cr.at[s])
+        for half in range(2):
+            turned = jnp.transpose(piece_all[half, pl.ds(2 * s, 2)].reshape(256, 256).astype(F32))
+            value_v[256 * half:256 * (half + 1), 256 * s:256 * (s + 1)] = turned.astype(BF16)
+
+    def az_sent(d, p):
+        landed(az_view(d, p), az_s.at[az_slot(d, p)])
+
+    def across_sent(b):
+        landed(wfull.at[0, pl.ds(0, REST if b == 8 else EARLY), :], ax_s.at[b])
 
     w_own.wait()
-    across(0, own_rows, fsdp, (0, 128))
+    across(0, fsdp, EARLY, REST, 8)
+    spread(0)
     az_send(1, 0)
     top_g = jnp.maximum(top_g, attention(1))
     cot_send(0)
@@ -485,52 +488,59 @@
     spread(-2)
     az_wait(3, 0)
     az_send(4, 0)
+    spread(3)
+    spread(-3)
+    landed(x_out, xs_sem)
+    for s in range(2):
+        cot_copies[s].wait_send()
+        for ring in stages[s][:2]:
+            ring.drain()
+    for d in (1, 2):
+        for p in range(2):
+            az_sent(d, p)
+    landed(pk1, p1s)
     for dz in (1, -1):
         across_wait(dz % NZ, 0)
         input_grad(z + dz)
     c_send(0)
     az_wait(3, 1)
+    across_wait(3, 0)
     az_send(4, 1)
-    spread(3)
-    spread(-3)
     peak_join(1, NY - 1, pk2, p2r)
     peak_send(2, [at(dz=dz) for dz in range(1, NZ)], pk3, p3s, p3r)
     c_send(1)
+    for s in range(2):
+        landed(zrecv.at[s, pl.ds(1, NZ - 1)], zs.at[s])
+        for ring in stages[s][2:]:
+            ring.drain()
+    landed(c_view(), cs.at[0])
+    landed(pk2, p2s)
+    for b in (0, 1, 2, 6, 7, 8):
+        across_sent(b)
     for dz in (2, -2):
         across_wait(dz % NZ, 0)
         input_grad(z + dz)
-    az_wait(4, 0)
-    spread(4)
-    v_send(0)
-    for dz in (3, -3):
-        across_wait(dz % NZ, 0)
-        input_grad(z + dz)
-    v_send(1)
+    v_turn(0)
+    across_wait(NZ - 3, 0)
+    input_grad(z + 3)
+    input_grad(z - 3)
+    az_sent(3, 0)
+    az_sent(3, 1)
+    across_sent(3)
+    across_sent(5)
+    v_turn(1)
     peak_join(2, NZ - 1, pk3, p3r)
     peak_out[...] = pk[3]
+    az_wait(4, 0)
     az_wait(4, 1)
-    across_wait(4, 0)
     input_grad(z + 4)
 
-    for b in range(9):
-        landed(wfull.at[0, pl.ds(0, 128), :], ax_s.at[b])
-    for d in range(1, 5):
-        for p in range(2):
-            landed(az_view(d, p), az_s.at[az_slot(d, p)])
-    for got, sem in ((pk1, p1s), (pk2, p2s), (pk3, p3s)):
-        landed(got, sem)
-    for s in range(2):
-        cot_copies[s].wait_send()
-        landed(zrecv.at[s, pl.ds(1, NZ - 1)], zs.at[s])
-        landed(zrecv.at[s, pl.ds(1, NZ - 1)], cs.at[s])
-    for ring in stages[0] + stages[1]:
-        ring.drain()
-
-    landed(x_out, xs_sem)
+    az_sent(4, 0)
+    az_sent(4, 1)
+    landed(c_view(), cs.at[1])
+    landed(pk3, p3s)
     landed(other_v, oth_s)
     landed(other_v, oth_r)
-    for copy in v_copies:
-        copy.wait()
 
 
 def hand_over(value, grad, peaks, value_out, grad_out, peaks_out, weight_out, sems):
@@ -564,18 +574,18 @@
         scratch_shapes=[
             vm((16, 2 * T, 256), BF16), vm((T, 4096), BF16), vm((T, KV), BF16), vm((T, 4096), BF16),
             vm((16, 256, KV), BF16), vm((2, T, KV), BF16), vm((256, 2 * T), BF16),
-            vm((2, NZ, 2, 2, 2, NY, 16, 256), BF16), vm((2, NZ, NY, 16, 256), BF16),
-            vm((2, NZ, 2, 2, 16, 256), BF16), vm((2, NZ, 2, 16, 256), BF16),
+            vm((2, 2, 2, NZ, NY, 16, 256), BF16), vm((2, NY, NZ, 2, 2, 16, 256), BF16),
+            vm((2, NY, NZ, 16, 256), BF16), vm((2, 2, 2, NZ, 16, 256), BF16), vm((2, NZ, 2, 16, 256), BF16),
             vm((2, 6, 4, NY, 16, 256), BF16), vm((2, 6, 4, 2, 2, 16, 256), BF16),
             vm((2, 2, 3, 4, 16, 256), BF16), vm((2, 2, 3, 4, 16, 256), BF16),
-            vm((2, NZ, 2, 16, 256), BF16), vm((2, 2, 16, 256), BF16), vm((4, 8, 16, 256), BF16),
+            vm((2, NZ, 2, 16, 256), BF16), vm((2, 2, 16, 256), BF16), vm((2, 4, 8, 16, 256), BF16),
             vm((16, T, 256), BF16),
             vm((4, 8, 128), F32), vm((7, 8, 128), F32), vm((3, 8, 128), F32), vm((7, 8, 128), F32),
             vm((16, T, 256), BF16),
             dma((5,)), dma, dma, dma, dma((2,)), dma, dma((9,)), dma((9,)), dma((8,)), dma((8,)),
             dma((2,)), dma((2,)), dma, dma, dma, dma, dma, dma,
             dma((2,)), dma((2, 6)), dma((2,)), dma((2, 6)), dma((2,)), dma((2, 2)), dma((2,)), dma((2, 2)),
-            dma((2,)), dma((2,)), dma((2,)), dma((2,)), dma, dma, dma((2,)), dma((2,)),
+            dma((2,)), dma((2,)), dma((2,)), dma((2,)), dma, dma,
         ],
         compiler_params=pltpu.CompilerParams(
             collective_id=0, has_side_effects=True, vmem_limit_bytes=60 << 20

time: 63.8 us -> 62.4 us (0.978)
  Pallas kernels: 63.1 us -> 61.6 us
    pallas_call x1, Pallas kernels: 60.7 us -> 59.2 us  [body(): pl.pallas_call(kernel, out_shape=(vm((512, KV), BF16), vm((T, D), BF16),...]
where the time goes in v4:
time: 62.4 us; the launch traced here: 62.3 us
  Pallas kernels  61.6 us (99%)
  between operations  0.64 us (1%)
    pallas_call x1, Pallas kernels, body(): pl.pallas_call(kernel, out_shape=(vm((512, KV), BF16), vm((T, D), BF16),...  59.2 us
    pallas_call x1, Pallas kernels, body(): pl.pallas_call(hand_over, out_shape=(jax.ShapeDtypeStruct((512, KV), BF16...  2.4 us

profile of v4, /device:TPU:1, one launch (start us, length us, event | category | flops | bytes accessed | tf_op | source)
XLA Modules:
  0.0 62.3 jit_solution(11716768474562713475)
XLA Ops:
  0.6 59.2 %value_backward.1 = (bf16[512,512]{1,0:T(8,128)(2,1)S(1)}, bf16[192,8192]{1,0:T(8,128)(2,1)S(1)}, f32[8,128]{1,0:T(8,128)S(1)}) custom-call(bf16[192,8192]{1,0:T(8,128)(2,1)} %x_hbm.1, bf16[192,4096]{1,0:T(8,128)(2,1)} %q_hbm.1, bf16[192,512]{1,0:T(8,128)(2,1)} %k_hbm.1, bf16[192,4096]{1,0:T(8,128)(2,1)} %g_hbm.1, bf16[512,512]{1,0:T(8,128)(2,1)} %w_hbm.1), custom_call_target="tpu_custom_call" | custom-call | tf_op jit(solution)/shard_map/value_backward/pallas_call | solution.py:565
  59.9 2.4 %hand_over.1 = (bf16[512,512]{1,0:T(8,128)(2,1)}, bf16[192,8192]{1,0:T(8,128)(2,1)}, f32[2]{0:T(128)}, f32[1]{0:T(128)}) custom-call(bf16[512,512]{1,0:T(8,128)(2,1)S(1)} %get-tuple-element.7.value, bf16[192,8192]{1,0:T(8,128)(2,1)S(1)} %get-tuple-element.8.grad, f32[8,128]{1,0:T(8,128)S(1)} %get-tuple-element.9.peaks), custom_call_target="tpu_custom_call" | custom-call | tf_op jit(solution)/shard_map/hand_over/pallas_call | solution.py:595

commit v5 on v4

--- a/solution.py
+++ b/solution.py
@@ -58,9 +58,6 @@
 
         lax.fori_loop(0, 4, add, 0)
 
-    def drain(self):
-        landed(self.bufs, self.send)
-
 
 LINE = [(dx, dc) for dx in range(NX) for dc in range(2) if (dx, dc) != (0, 0)]
 GROUP = [(dx, dy, dc) for dx in (2, 0) for dy in (2, 1, 3, 0) for dc in (1, 0) if (dx, dy, dc) != (0, 0, 0)]
@@ -122,9 +119,6 @@
             return 0
 
         lax.fori_loop(0, 4, add, 0)
-
-    def drain(self):
-        landed(self.bufs, self.send)
 
 
 def kernel(
@@ -222,7 +216,7 @@
         for i, dx in enumerate((1, -1)):
             view = wfull.at[block, pl.ds(base + i * (count // 2), count // 2), :]
             copy = pltpu.make_async_remote_copy(
-                src_ref=view, dst_ref=view, send_sem=ax_s.at[sem], recv_sem=ax_r.at[sem],
+                src_ref=view, dst_ref=view, send_sem=ax_s, recv_sem=ax_r.at[sem],
                 device_id=at(dx=dx), device_id_type=MESH,
             )
             copy.start()
@@ -257,7 +251,7 @@
             slot = az_slot(d, p)
             rows = pl.ds(base, count)
             copy = pltpu.make_async_remote_copy(
-                src_ref=wfull.at[block, rows, :], dst_ref=wfull.at[block, rows, :], send_sem=az_s.at[slot], recv_sem=az_r.at[slot],
+                src_ref=wfull.at[block, rows, :], dst_ref=wfull.at[block, rows, :], send_sem=az_s, recv_sem=az_r.at[slot],
                 device_id=at(dz=dz), device_id_type=MESH,
             )
             copy.start()
@@ -270,7 +264,7 @@
     def cot_send(s):
         cols = pl.ds(256 * s, 256)
         cot_copies.append(pltpu.make_async_remote_copy(
-            src_ref=cot.at[0, :, cols], dst_ref=cot.at[1, :, cols], send_sem=cot_s.at[s], recv_sem=cot_r.at[s],
+            src_ref=cot.at[0, :, cols], dst_ref=cot.at[1, :, cols], send_sem=cot_s, recv_sem=cot_r.at[s],
             device_id=mate, device_id_type=MESH,
         ))
         cot_copies[-1].start()
@@ -339,10 +333,10 @@
             fin[s, i, 1] = v.astype(BF16)
 
         return (
-            Ring(xp, xm, take1, put1, r1.at[s], r1s.at[s], r1r.at[s]),
-            Ring(yp, ym, take2, put2, r2.at[s], r2s.at[s], r2r.at[s]),
-            Straight([at(dy=i) for i in (1, 2, 3)], take3, put3, r3.at[s], r3s.at[s], r3r.at[s]),
-            Straight([at(dx=i) for i in (1, 2, 3)], take4, put4, r4.at[s], r4s.at[s], r4r.at[s]),
+            Ring(xp, xm, take1, put1, r1.at[s], r1s, r1r.at[s]),
+            Ring(yp, ym, take2, put2, r2.at[s], r2s, r2r.at[s]),
+            Straight([at(dy=i) for i in (1, 2, 3)], take3, put3, r3.at[s], r3s, r3r.at[s]),
+            Straight([at(dx=i) for i in (1, 2, 3)], take4, put4, r4.at[s], r4s, r4r.at[s]),
         )
 
     stages = [rings(0), rings(1)]
@@ -383,7 +377,7 @@
         for i in (4, 3, 5, 2, 6, 1, 7):
             zd = lax.rem(z + i, NZ)
             copy = pltpu.make_async_remote_copy(
-                src_ref=fin.at[s, zd], dst_ref=zrecv.at[s, i], send_sem=zs.at[s], recv_sem=zr.at[s],
+                src_ref=fin.at[s, zd], dst_ref=zrecv.at[s, i], send_sem=zs, recv_sem=zr.at[s],
                 device_id=at(dz=i), device_id_type=MESH,
             )
             copy.start()
@@ -398,7 +392,7 @@
         piece[s] = (total * (1.0 / 256.0)).astype(BF16)
         for dx, dy, dc in GROUP:
             copy = pltpu.make_async_remote_copy(
-                src_ref=piece.at[s], dst_ref=piece_all.at[c, pl.ds(2 * s, 2), j], send_sem=cs.at[s],
+                src_ref=piece.at[s], dst_ref=piece_all.at[c, pl.ds(2 * s, 2), j], send_sem=cs,
                 recv_sem=cr.at[s], device_id=at(dx=dx, dy=dy, dc=dc), device_id_type=MESH,
             )
             copy.start()
@@ -434,12 +428,6 @@
         for half in range(2):
             turned = jnp.transpose(piece_all[half, pl.ds(2 * s, 2)].reshape(256, 256).astype(F32))
             value_v[256 * half:256 * (half + 1), 256 * s:256 * (s + 1)] = turned.astype(BF16)
-
-    def az_sent(d, p):
-        landed(az_view(d, p), az_s.at[az_slot(d, p)])
-
-    def across_sent(b):
-        landed(wfull.at[0, pl.ds(0, REST if b == 8 else EARLY), :], ax_s.at[b])
 
     w_own.wait()
     across(0, fsdp, EARLY, REST, 8)
@@ -491,13 +479,6 @@
     spread(3)
     spread(-3)
     landed(x_out, xs_sem)
-    for s in range(2):
-        cot_copies[s].wait_send()
-        for ring in stages[s][:2]:
-            ring.drain()
-    for d in (1, 2):
-        for p in range(2):
-            az_sent(d, p)
     landed(pk1, p1s)
     for dz in (1, -1):
         across_wait(dz % NZ, 0)
@@ -509,14 +490,7 @@
     peak_join(1, NY - 1, pk2, p2r)
     peak_send(2, [at(dz=dz) for dz in range(1, NZ)], pk3, p3s, p3r)
     c_send(1)
-    for s in range(2):
-        landed(zrecv.at[s, pl.ds(1, NZ - 1)], zs.at[s])
-        for ring in stages[s][2:]:
-            ring.drain()
-    landed(c_view(), cs.at[0])
     landed(pk2, p2s)
-    for b in (0, 1, 2, 6, 7, 8):
-        across_sent(b)
     for dz in (2, -2):
         across_wait(dz % NZ, 0)
         input_grad(z + dz)
@@ -524,10 +498,6 @@
     across_wait(NZ - 3, 0)
     input_grad(z + 3)
     input_grad(z - 3)
-    az_sent(3, 0)
-    az_sent(3, 1)
-    across_sent(3)
-    across_sent(5)
     v_turn(1)
     peak_join(2, NZ - 1, pk3, p3r)
     peak_out[...] = pk[3]
@@ -535,9 +505,13 @@
     az_wait(4, 1)
     input_grad(z + 4)
 
-    az_sent(4, 0)
-    az_sent(4, 1)
-    landed(c_view(), cs.at[1])
+    landed(wfull.at[pl.ds(0, 11)], az_s)
+    landed(wfull.at[pl.ds(0, 4)], ax_s)
+    landed(cot.at[0], cot_s)
+    for bufs, sem in ((r1, r1s), (r2, r2s), (r3, r3s), (r4, r4s)):
+        landed(bufs, sem)
+    landed(zrecv.at[:, pl.ds(1, NZ - 1)], zs)
+    landed(wfull.at[pl.ds(0, 2), pl.ds(0, 16 * len(GROUP)), :], cs)
     landed(pk3, p3s)
     landed(other_v, oth_s)
     landed(other_v, oth_r)
@@ -582,10 +556,10 @@
             vm((16, T, 256), BF16),
             vm((4, 8, 128), F32), vm((7, 8, 128), F32), vm((3, 8, 128), F32), vm((7, 8, 128), F32),
             vm((16, T, 256), BF16),
-            dma((5,)), dma, dma, dma, dma((2,)), dma, dma((9,)), dma((9,)), dma((8,)), dma((8,)),
-            dma((2,)), dma((2,)), dma, dma, dma, dma, dma, dma,
-            dma((2,)), dma((2, 6)), dma((2,)), dma((2, 6)), dma((2,)), dma((2, 2)), dma((2,)), dma((2, 2)),
-            dma((2,)), dma((2,)), dma((2,)), dma((2,)), dma, dma,
+            dma((5,)), dma, dma, dma, dma((2,)), dma, dma, dma((9,)), dma, dma((8,)),
+            dma, dma((2,)), dma, dma, dma, dma, dma, dma,
+            dma, dma((2, 6)), dma, dma((2, 6)), dma, dma((2, 2)), dma, dma((2, 2)),
+            dma, dma((2,)), dma, dma((2,)), dma, dma,
         ],
         compiler_params=pltpu.CompilerParams(
             collective_id=0, has_side_effects=True, vmem_limit_bytes=60 << 20

time: 62.4 us -> 62.2 us (level)
  no operation moved by 1% of the time
where the time goes in v5:
time: 62.2 us; the launch traced here: 62.1 us
  Pallas kernels  61.4 us (99%)
  between operations  0.64 us (1%)
    pallas_call x1, Pallas kernels, body(): pl.pallas_call(kernel, out_shape=(vm((512, KV), BF16), vm((T, D), BF16),...  59 us
    pallas_call x1, Pallas kernels, body(): pl.pallas_call(hand_over, out_shape=(jax.ShapeDtypeStruct((512, KV), BF16...  2.4 us

profile of v5, /device:TPU:1, one launch (start us, length us, event | category | flops | bytes accessed | tf_op | source)
XLA Modules:
  0.0 62.1 jit_solution(11750057146156511780)
XLA Ops:
  0.6 59.0 %value_backward.1 = (bf16[512,512]{1,0:T(8,128)(2,1)S(1)}, bf16[192,8192]{1,0:T(8,128)(2,1)S(1)}, f32[8,128]{1,0:T(8,128)S(1)}) custom-call(bf16[192,8192]{1,0:T(8,128)(2,1)} %x_hbm.1, bf16[192,4096]{1,0:T(8,128)(2,1)} %q_hbm.1, bf16[192,512]{1,0:T(8,128)(2,1)} %k_hbm.1, bf16[192,4096]{1,0:T(8,128)(2,1)} %g_hbm.1, bf16[512,512]{1,0:T(8,128)(2,1)} %w_hbm.1), custom_call_target="tpu_custom_call" | custom-call | tf_op jit(solution)/shard_map/value_backward/pallas_call | solution.py:539
  59.7 2.4 %hand_over.1 = (bf16[512,512]{1,0:T(8,128)(2,1)}, bf16[192,8192]{1,0:T(8,128)(2,1)}, f32[2]{0:T(128)}, f32[1]{0:T(128)}) custom-call(bf16[512,512]{1,0:T(8,128)(2,1)S(1)} %get-tuple-element.7.value, bf16[192,8192]{1,0:T(8,128)(2,1)S(1)} %get-tuple-element.8.grad, f32[8,128]{1,0:T(8,128)S(1)} %get-tuple-element.9.peaks), custom_call_target="tpu_custom_call" | custom-call | tf_op jit(solution)/shard_map/hand_over/pallas_call | solution.py:569
